TPU v7x, 32 devices: a whole 2x2x4 slice. The times are simulated.
32 devices in a mesh: strips: 2 (over y), wave: 4 (over x, core), cols: 4 (over z).
Axes of the slice: x: 2, y: 2, z: 4, core: 2. Of those that a mesh axis runs over, the one named last changes fastest.
Arguments:
- frames: bfloat16 [1024, 32, 4096], P('wave', 'strips', 'cols'), parts along dimension 1, may hold values from -6 to 6
- wavenumbers: float32 [1024], replicated, may hold values from 0 to 1
- band_start: int32 [6], replicated, may hold values from 0 to 384
- aperture_offset: int32 [64], P(('strips', 'cols')), parts along dimension 0, may hold values from 0 to 15
- aperture_count: int32 [64], P(('strips', 'cols')), parts along dimension 0, may hold values from 4 to 16
- reference_pixels: int32 [512], P('strips'), parts along dimension 0, may hold values from 0 to 65535, as said below
Outputs:
- cavity_maps: bfloat16 [6, 2, 128, 32, 4096], P(None, None, None, ('strips', 'wave'), 'cols'), parts along dimension 3
There are 2 independent parts, one for each index of `strips`. A program takes and returns all parts, laid end to end along the dimension named above; an argument that names none is the same for every part. Nothing has to cross between parts.
Inputs may be any that keep to these rules, and one draw needn't show every extreme that they name: `reference_pixels`: the indices are distinct.
All inputs are finite; a program needn't handle non-finite values.
Results may differ from a plain program's by a relative error of at most 0.0056.
Values may be sent and summed in bfloat16 or wider, within the bound.
A program may use at most 128 MiB of HBM per device.

v0:
```python
import math

import jax
import jax.numpy as jnp
from jax import lax
from jax.sharding import PartitionSpec as P

NB = 128


TWO_PI = 2.0 * math.pi
EPS = 1e-06


def table_block(wavenumbers, band_start, first_row, count, bins_band, frame_total):
    rows = first_row + jnp.arange(count, dtype=jnp.int32)
    cavity = rows // (2 * bins_band)
    imag_part = rows // bins_band % 2
    offset_bin = rows % bins_band
    cav_ids = jnp.arange(band_start.shape[0], dtype=jnp.int32)
    start_of = jnp.sum(
        jnp.where(cavity[:, None] == cav_ids[None, :], band_start[None, :], 0), axis=1
    )
    bins = (start_of + offset_bin).astype(jnp.float32)
    frame_pos = jnp.arange(frame_total, dtype=jnp.float32)
    window = (0.5 - 0.5 * jnp.cos(TWO_PI * (frame_pos + 0.5) / frame_total)) / math.sqrt(
        frame_total
    )
    angle_mat = bins[:, None] * wavenumbers[None, :] * TWO_PI
    value = (
        jnp.where(imag_part[:, None] == 0, jnp.cos(angle_mat), -jnp.sin(angle_mat))
        * window[None, :]
    )
    return value.astype(jnp.bfloat16)


def shards(frames, wavenumbers, band_start, aperture_offset, aperture_count, reference_pixels):
    frame_dev, rows_all, cols_dev = frames.shape
    frame_total = wavenumbers.shape[0]
    ncav = band_start.shape[0]
    total_rows = 2 * ncav * NB
    blocks = lax.map(
        lambda c: table_block(wavenumbers, band_start, c * 2 * NB, 2 * NB, NB, frame_total),
        jnp.arange(ncav, dtype=jnp.int32),
    )
    table = blocks.reshape(total_rows, frame_total)
    block_cols = cols_dev // aperture_offset.shape[0]
    off_cols = jnp.repeat(aperture_offset, block_cols)
    cnt_cols = jnp.repeat(aperture_count, block_cols)
    row_ids = jnp.arange(rows_all, dtype=jnp.int32)[:, None]
    valid = (
        (row_ids >= off_cols[None, :]) & (row_ids < off_cols[None, :] + cnt_cols[None, :])
    ).astype(jnp.bfloat16)
    masked = frames * valid[None, :, :]
    piece = lax.all_to_all(masked, "wave", split_axis=1, concat_axis=0, tiled=True)
    nframe, nrow, nitem = piece.shape
    flat = piece.reshape(nframe, nrow * nitem)
    product = jnp.dot(table, flat, preferred_element_type=jnp.float32)
    spectra = product.reshape(ncav, 2, NB, nrow, nitem)
    rows_dev = spectra.shape[3]
    width_all = cols_dev * lax.axis_size("cols")
    rows_global = lax.axis_index("wave") * rows_dev + jnp.arange(rows_dev, dtype=jnp.int32)
    cols_global = lax.axis_index("cols") * cols_dev + jnp.arange(cols_dev, dtype=jnp.int32)
    flat_index = rows_global[:, None] * width_all + cols_global[None, :]
    selected = jnp.sum(
        (reference_pixels[:, None, None] == flat_index[None, :, :]).astype(jnp.float32), axis=0
    )
    middle = spectra[:, :, NB // 2]
    part_re = jnp.sum(middle[:, 0] * selected[None], axis=(1, 2))
    part_im = jnp.sum(middle[:, 1] * selected[None], axis=(1, 2))
    part_power = jnp.sum(
        (middle[:, 0] * middle[:, 0] + middle[:, 1] * middle[:, 1]) * selected[None], axis=(1, 2)
    )
    ref_re, ref_im, power = lax.psum((part_re, part_im, part_power), ("wave", "cols"))
    scale = 1.0 / jnp.sqrt(power + EPS)
    real_part = spectra[:, 0]
    imag_part = spectra[:, 1]
    out_re = (
        real_part * ref_re[:, None, None, None] + imag_part * ref_im[:, None, None, None]
    ) * scale[:, None, None, None]
    out_im = (
        imag_part * ref_re[:, None, None, None] - real_part * ref_im[:, None, None, None]
    ) * scale[:, None, None, None]
    return jnp.stack([out_re, out_im], axis=1).astype(jnp.bfloat16)


def solution(mesh):
    placed = (
        P("wave", "strips", "cols"),
        P(),
        P(),
        P(("strips", "cols")),
        P(("strips", "cols")),
        P("strips"),
    )
    return jax.shard_map(
        shards,
        mesh=mesh,
        in_specs=placed,
        out_specs=P(None, None, None, ("strips", "wave"), "cols"),
        check_vma=False,
    )
```

profile of v0, /device:TPU:0, one launch (start us, length us, event | category | flops | bytes accessed | tf_op | source)
XLA Modules:
  0.0 216.6 jit_solution(6712594364718436857)
XLA Ops:
  0.0 0.7 broadcast_bitcast_fusion
  0.7 0.7 bitcast_add_fusion
  1.5 16.0 %copy_multiply_fusion = bf16[256,16,1024]{2,0,1:T(8,128)(2,1)} fusion(bf16[256,16,1024]{2,1,0:T(8,128)(2,1)} %param.8, bf16[16,1024]{1,0:T(8,128)(2,1)S(1)} %fusion.7), kind=kLoop, calls=%fused_computation.27 | loop fusion | flops 4194304 | bytes 16809984 | tf_op jit(solution)/shard_map/mul | solution.py:54
  17.5 6.0 %all-to-all-start = ((bf16[256,16,1024]{2,0,1:T(8,128)(2,1)}), bf16[256,16,1024]{2,0,1:T(8,128)(2,1)}, u32[]{:S(2)}, u32[]{:S(2)}) async-start(bf16[256,16,1024]{2,0,1:T(8,128)(2,1)} %copy_multiply_fusion), calls=%async_computation | async-start | bytes 16777216 | tf_op jit(solution)/shard_map/all_to_all | solution.py:55
  23.6 0.5 convert_reduce_fusion
  24.1 33.7 %while.13 = (s32[]{:T(128)}, bf16[6,256,1024]{2,1,0:T(8,128)(2,1)S(1)}, s32[6]{0:T(128)S(1)}, s32[6]{0:T(128)S(1)}, f32[1024]{0:T(1024)S(1)}, /*index=5*/s32[]{:T(128)}, s32[1]{0:T(128)}) while((s32[]{:T(128)}, bf16[6,256,1024]{2,1,0:T(8,128)(2,1)S(1)}, s32[6]{0:T(128)S(1)}, s32[6]{0:T(128)S(1)}, f32[1024]{0:T(1024)S(1)}, ...), condition=%wide.region_2.3_spmd, body=%wide.region_0.2_spmd.sunk | while | flops 1597187 | bytes 543637 | solution.py:42
  24.1 0.6 dynamic_slice.9
  25.3 0.1 select_reduce_fusion.2
  25.5 4.3 %fusion.16 = bf16[6,256,1024]{2,1,0:T(8,128)(2,1)S(1)} fusion(bf16[6,256,1024]{2,1,0:T(8,128)(2,1)S(1)} %get-tuple-element.168, s32[]{:T(128)S(6)} %copy.30, f32[1024]{0:T(1024)S(1)} %subtract_multiply_fusion.2, f32[1024]{0:T(1024)S(1)} %get-tuple-element.178, f32[256]{0:T(256)S(1)} %fusion.14, pred[256]{0:T(512)(128)(4,1)S(1)} %fusion.15), kind=kLoop, calls=%fused_computation.1.clone.1 | loop fusion | flops 1572864 | bytes 534020 | tf_op jit(solution)/shard_map/while/body/jit(dynamic_update_index_in_dim)/dynamic_update_slice | solution.py:42
  29.8 0.6 dynamic_slice.9
  30.9 0.1 select_reduce_fusion.2
  31.1 4.3 %fusion.16 = bf16[6,256,1024]{2,1,0:T(8,128)(2,1)S(1)} fusion(bf16[6,256,1024]{2,1,0:T(8,128)(2,1)S(1)} %get-tuple-element.168, s32[]{:T(128)S(6)} %copy.30, f32[1024]{0:T(1024)S(1)} %subtract_multiply_fusion.2, f32[1024]{0:T(1024)S(1)} %get-tuple-element.178, f32[256]{0:T(256)S(1)} %fusion.14, pred[256]{0:T(512)(128)(4,1)S(1)} %fusion.15), kind=kLoop, calls=%fused_computation.1.clone.1 | loop fusion | flops 1572864 | bytes 534020 | tf_op jit(solution)/shard_map/while/body/jit(dynamic_update_index_in_dim)/dynamic_update_slice | solution.py:42
  35.4 0.6 dynamic_slice.9
  36.6 0.1 select_reduce_fusion.2
  36.7 4.3 %fusion.16 = bf16[6,256,1024]{2,1,0:T(8,128)(2,1)S(1)} fusion(bf16[6,256,1024]{2,1,0:T(8,128)(2,1)S(1)} %get-tuple-element.168, s32[]{:T(128)S(6)} %copy.30, f32[1024]{0:T(1024)S(1)} %subtract_multiply_fusion.2, f32[1024]{0:T(1024)S(1)} %get-tuple-element.178, f32[256]{0:T(256)S(1)} %fusion.14, pred[256]{0:T(512)(128)(4,1)S(1)} %fusion.15), kind=kLoop, calls=%fused_computation.1.clone.1 | loop fusion | flops 1572864 | bytes 534020 | tf_op jit(solution)/shard_map/while/body/jit(dynamic_update_index_in_dim)/dynamic_update_slice | solution.py:42
  41.0 0.6 dynamic_slice.9
  42.2 0.1 select_reduce_fusion.2
  42.3 4.3 %fusion.16 = bf16[6,256,1024]{2,1,0:T(8,128)(2,1)S(1)} fusion(bf16[6,256,1024]{2,1,0:T(8,128)(2,1)S(1)} %get-tuple-element.168, s32[]{:T(128)S(6)} %copy.30, f32[1024]{0:T(1024)S(1)} %subtract_multiply_fusion.2, f32[1024]{0:T(1024)S(1)} %get-tuple-element.178, f32[256]{0:T(256)S(1)} %fusion.14, pred[256]{0:T(512)(128)(4,1)S(1)} %fusion.15), kind=kLoop, calls=%fused_computation.1.clone.1 | loop fusion | flops 1572864 | bytes 534020 | tf_op jit(solution)/shard_map/while/body/jit(dynamic_update_index_in_dim)/dynamic_update_slice | solution.py:42
  46.6 0.6 dynamic_slice.9
  48.0 4.3 %fusion.16 = bf16[6,256,1024]{2,1,0:T(8,128)(2,1)S(1)} fusion(bf16[6,256,1024]{2,1,0:T(8,128)(2,1)S(1)} %get-tuple-element.168, s32[]{:T(128)S(6)} %copy.30, f32[1024]{0:T(1024)S(1)} %subtract_multiply_fusion.2, f32[1024]{0:T(1024)S(1)} %get-tuple-element.178, f32[256]{0:T(256)S(1)} %fusion.14, pred[256]{0:T(512)(128)(4,1)S(1)} %fusion.15), kind=kLoop, calls=%fused_computation.1.clone.1 | loop fusion | flops 1572864 | bytes 534020 | tf_op jit(solution)/shard_map/while/body/jit(dynamic_update_index_in_dim)/dynamic_update_slice | solution.py:42
  52.2 0.6 dynamic_slice.9
  53.6 4.3 %fusion.16 = bf16[6,256,1024]{2,1,0:T(8,128)(2,1)S(1)} fusion(bf16[6,256,1024]{2,1,0:T(8,128)(2,1)S(1)} %get-tuple-element.168, s32[]{:T(128)S(6)} %copy.30, f32[1024]{0:T(1024)S(1)} %subtract_multiply_fusion.2, f32[1024]{0:T(1024)S(1)} %get-tuple-element.178, f32[256]{0:T(256)S(1)} %fusion.14, pred[256]{0:T(512)(128)(4,1)S(1)} %fusion.15), kind=kLoop, calls=%fused_computation.1.clone.1 | loop fusion | flops 1572864 | bytes 534020 | tf_op jit(solution)/shard_map/while/body/jit(dynamic_update_index_in_dim)/dynamic_update_slice | solution.py:42
  57.9 59.4 %all-to-all-done = bf16[256,16,1024]{2,0,1:T(8,128)(2,1)} async-done(((bf16[256,16,1024]{2,0,1:T(8,128)(2,1)}), bf16[256,16,1024]{2,0,1:T(8,128)(2,1)}, u32[]{:S(2)}, u32[]{:S(2)}) %all-to-all-start) | async-done | bytes 8388640 | tf_op jit(solution)/shard_map/all_to_all | solution.py:55
  117.2 13.8 %copy.15 = bf16[4,256,4,1024]{1,0,3,2:T(4,128)(2,1)} copy(bf16[4,256,4,1024]{3,1,2,0:T(8,128)(2,1)} %bitcast.7) | data formatting | bytes 16777216 | tf_op jit(solution)/shard_map/all_to_all | solution.py:55
  131.0 9.3 %copy.23 = bf16[512,8,4,256]{3,1,2,0:T(8,128)(2,1)} copy(bf16[512,8,4,256]{3,2,1,0:T(4,128)(2,1)} %bitcast.49) | data formatting | bytes 16777216
  140.3 20.4 %fusion.8 = f32[6,2,128,4,1024]{4,2,3,1,0:T(8,128)} fusion(bf16[6,2,128,1024,1]{3,2,4,1,0:T(8,128)(2,1)S(1)} %bitcast.52, bf16[4,1024,1024,1,1]{2,1,0,4,3:T(8,128)(2,1)} %bitcast.50), kind=kOutput, calls=%fused_computation.45 | convolution fusion | flops 12884901888 | bytes 36700160 | tf_op jit(solution)/shard_map/dot_general | solution.py:58
  160.7 1.5 slice.25
  162.3 0.2 multiply_reduce_fusion.2
  162.5 33.4 %all-reduce = (f32[6]{0:T(128)S(1)}, f32[6]{0:T(128)S(1)}, f32[6]{0:T(128)S(1)}) all-reduce(f32[6]{0:T(128)S(1)} %get-tuple-element.112, f32[6]{0:T(128)S(1)} %get-tuple-element.113, f32[6]{0:T(128)S(1)} %get-tuple-element.111), channel_id=1, replica_groups=mesh['strips'=2,'wave'=4,'cols'=4] {'wave','cols'}, use_global_device_ids=true, to_apply=%region_9.10 | all-reduce | flops 18 | bytes 144 | tf_op jit(solution)/shard_map/psum | solution.py:74
  195.9 10.1 %multiply_convert_fusion.2 = (bf16[6,1,128,4,1024]{4,2,3,1,0:T(8,128)(2,1)S(1)}, bf16[6,1,128,4,1024]{4,2,3,1,0:T(8,128)(2,1)S(1)}) fusion(f32[6,2,128,4,1024]{4,2,3,1,0:T(8,128)} %fusion.8, f32[6]{0:T(128)S(1)} %add_rsqrt_fusion, f32[6]{0:T(128)S(1)} %get-tuple-element.125, f32[6]{0:T(128)S(1)} %get-tuple-element.126), kind=kLoop, calls=%fused_computation.26 | loop fusion | flops 31457280 | bytes 37748808 | tf_op jit(solution)/shard_map/convert
  205.9 1.2 pad_maximum_fusion
  207.2 9.4 %copy.17 = bf16[6,2,128,4,1024]{4,3,2,1,0:T(4,128)(2,1)} copy(bf16[6,2,128,4,1024]{4,2,3,1,0:T(8,128)(2,1)S(1)} %pad_maximum_fusion) | data formatting | bytes 25165824 | tf_op jit(solution)/shard_map/stack | solution.py:84
  (40 shorter events, 0.9 us)
Async XLA Ops:
  17.5 6.1 %copy-start.1 = (s32[256]{0:T(256)S(1)}, s32[256]{0:T(256)}, u32[]{:S(2)}) copy-start(s32[256]{0:T(256)} %param.13) | copy-start | bytes 3076
  17.5 6.6 %copy-start = (s32[6]{0:T(128)S(1)}, s32[6]{0:T(128)}, u32[]{:S(2)}) copy-start(s32[6]{0:T(128)} %param.10) | copy-start | bytes 76
  17.5 6.7 %copy-start.2 = (f32[1024]{0:T(1024)S(1)}, f32[1024]{0:T(1024)}, u32[]{:S(2)}) copy-start(f32[1024]{0:T(1024)} %param.9) | copy-start | bytes 12292
  17.5 99.7 %all-to-all-start = ((bf16[256,16,1024]{2,0,1:T(8,128)(2,1)}), bf16[256,16,1024]{2,0,1:T(8,128)(2,1)}, u32[]{:S(2)}, u32[]{:S(2)}) async-start(bf16[256,16,1024]{2,0,1:T(8,128)(2,1)} %copy_multiply_fusion), calls=%async_computation | async-start | bytes 16777216 | tf_op jit(solution)/shard_map/all_to_all | solution.py:55
where the time goes:
time: 217 us
  waiting for transfers between devices  59.4 us (27%)
  other arithmetic  55.6 us (26%)
  local copies, waits for them, and re-layouts  38.1 us (18%)
  blocking collectives  33.4 us (15%)
  matrix products  20.4 us (9%)
  starting transfers between devices  5.97 us (3%)
  loops' own time  3.64 us (2%)
    all_to_all x1, waiting for transfers between devices, shards(): lax.all_to_all(masked, 'wave', split_axis=1, concat_axis=0, tiled=True)  59.4 us
    psum x1, blocking collectives, shards(): lax.psum((part_re, part_im, part_power), ('wave', 'cols'))  33.4 us
    dynamic_update_slice x6, other arithmetic, shards(): lax.map(lambda c: table_block(wavenumbers, band_start, c * 2 * NB, 2 * NB...  25.6 us
    dot_general x1, matrix products, shards(): product = jnp.dot(table, flat, preferred_element_type=jnp.float32)  20.4 us
    mul x1, other arithmetic, shards(): masked = frames * valid[None, :, :]  16 us
    all_to_all x1, local copies, waits for them, and re-layouts, shards(): lax.all_to_all(masked, 'wave', split_axis=1, concat_axis=0, tiled=True)  13.8 us
    another operation x1, other arithmetic  10.1 us
    unnamed x8, local copies, waits for them, and re-layouts  9.4 us
  transfers between devices with their start and end apart: 1, of which 1 were waited for; matrix products, arithmetic and copies ran while one was open for 14% of the time, Pallas kernels for 0%

commit v1 on v0

v1 whole, which is shorter than its diff:
```python
import functools
import math

import jax
import jax.numpy as jnp
from jax import lax
from jax.experimental import pallas as pl
from jax.experimental.pallas import tpu as pltpu
from jax.sharding import PartitionSpec as P

NB = 128
TWO_PI = 2.0 * math.pi
EPS = 1e-06
LANES = 128
VMEM_LIMIT = 48 * 1024 * 1024


def partner(me, step, n):
    if n & (n - 1) == 0:
        return me ^ step
    return (me + step) % n


def source(me, step, n):
    if n & (n - 1) == 0:
        return me ^ step
    return (me + n - step) % n


def send(value, step, n):
    return lax.ppermute(value, "wave", [(i, partner(i, step, n)) for i in range(n)])


def total_over(value, axis):
    n = lax.axis_size(axis)
    if n & (n - 1):
        return lax.psum(value, axis)
    step = 1
    while step < n:
        value = value + lax.ppermute(value, axis, [(i, i ^ step) for i in range(n)])
        step *= 2
    return value


def prep_kernel(n, rows_dev, chunk, width_all, block_cols, pos_ref, off_ref, cnt_ref, x_ref, pix_ref, *rest):
    outs, picked_ref, wide = rest[:n], rest[n], rest[n + 1]
    frames, rows_all, width = x_ref.shape
    pieces = width // LANES
    for b in range(pieces):
        wide[b] = x_ref[:, :, b * LANES:(b + 1) * LANES].astype(jnp.float32).reshape(
            frames * rows_all, LANES
        )
    me = pos_ref[0]
    first_col = pos_ref[1] + chunk * width
    pix = pix_ref[...]
    total = jnp.zeros((frames, pix.shape[1]), jnp.float32)
    for step in range(n):
        first_row = partner(me, step, n) * rows_dev
        for r in range(rows_dev):
            row = first_row + r
            for b in range(pieces):
                block = (chunk * width + b * LANES) // block_cols
                start = off_ref[block]
                good = (row >= start) & (row < start + cnt_ref[block])
                part = wide[b, pl.ds(row, frames, stride=rows_all), :]
                part = jnp.where(good, part, 0.0)
                outs[step][r, :, b * LANES:(b + 1) * LANES] = part.astype(jnp.bfloat16)
            local = pix - (row * width_all + first_col)
            hot = lax.broadcasted_iota(jnp.int32, (width, pix.shape[1]), 0) == local
            hot = jnp.where(hot, 1.0, 0.0).astype(jnp.bfloat16)
            total += jnp.dot(outs[step][r], hot, preferred_element_type=jnp.float32)
    picked_ref[...] = total


def prep(n, rows_dev, chunk, width, width_all, block_cols, pos, off, cnt, frames, pix):
    frame_dev, rows_all, _ = frames.shape
    npix = pix.shape[1]
    piece = jax.ShapeDtypeStruct((rows_dev, frame_dev, width), jnp.bfloat16)
    return pl.pallas_call(
        functools.partial(prep_kernel, n, rows_dev, chunk, width_all, block_cols),
        out_shape=[piece] * n + [jax.ShapeDtypeStruct((frame_dev, npix), jnp.float32)],
        grid_spec=pltpu.PrefetchScalarGridSpec(
            num_scalar_prefetch=3,
            grid=(1,),
            in_specs=[
                pl.BlockSpec((frame_dev, rows_all, width), lambda i, *_: (0, 0, chunk)),
                pl.BlockSpec((1, npix), lambda i, *_: (0, 0)),
            ],
            out_specs=[pl.BlockSpec(piece.shape, lambda i, *_: (0, 0, 0))] * n
            + [pl.BlockSpec((frame_dev, npix), lambda i, *_: (0, 0))],
            scratch_shapes=[pltpu.VMEM((width // LANES, frame_dev * rows_all, LANES), jnp.float32)],
        ),
        compiler_params=pltpu.CompilerParams(vmem_limit_bytes=VMEM_LIMIT),
        cost_estimate=pl.CostEstimate(flops=1024, bytes_accessed=1024, transcendentals=0),
        name="prep",
    )(pos, off, cnt, frames, pix)


def band_kernel(n, coef_ref, table_ref, *rest):
    pieces, out_ref, flat, mixed = rest[:n], rest[-3], rest[-2], rest[-1]
    rows_dev, frame_dev, width = pieces[0].shape
    nb = table_ref.shape[2]
    cav = pl.program_id(0)

    @pl.when(cav == 0)
    def _():
        for r in range(rows_dev):
            for i in range(n):
                flat[r, i * frame_dev:(i + 1) * frame_dev, :] = pieces[i][r]

    ca = coef_ref[0, cav]
    cb = coef_ref[1, cav]
    for r in range(rows_dev):
        table = table_ref[0].reshape(2 * nb, table_ref.shape[3])
        spec = jnp.dot(table, flat[r], preferred_element_type=jnp.float32)
        re, im = spec[:nb], spec[nb:]
        both = (re * ca + im * cb, im * ca - re * cb)
        for b in range(width // LANES):
            for q in range(2):
                mixed[q, b, pl.ds(r, nb, stride=rows_dev), :] = both[q][:, b * LANES:(b + 1) * LANES]
    for b in range(width // LANES):
        for q in range(2):
            value = mixed[q, b].reshape(nb, rows_dev, LANES).astype(jnp.bfloat16)
            out_ref[0, q, :, :, b * LANES:(b + 1) * LANES] = value


def band(n, chunk, cols_dev, coef, table, pieces, prev):
    rows_dev, frame_dev, width = pieces[0].shape
    ncav, _, nb, frame_total = table.shape
    out = jax.ShapeDtypeStruct((ncav, 2, nb, rows_dev, cols_dev), jnp.bfloat16)
    extra = [] if prev is None else [prev]
    return pl.pallas_call(
        functools.partial(band_kernel, n),
        out_shape=out,
        grid=(ncav,),
        in_specs=[
            pl.BlockSpec(memory_space=pltpu.SMEM),
            pl.BlockSpec((1, 2, nb, frame_total), lambda c: (c, 0, 0, 0)),
        ]
        + [pl.BlockSpec((rows_dev, frame_dev, width), lambda c: (0, 0, 0))] * n
        + [pl.BlockSpec(memory_space=pl.ANY)] * len(extra),
        out_specs=pl.BlockSpec((1, 2, nb, rows_dev, width), lambda c: (c, 0, 0, 0, chunk)),
        scratch_shapes=[
            pltpu.VMEM((rows_dev, frame_total, width), jnp.bfloat16),
            pltpu.VMEM((2, width // LANES, nb * rows_dev, LANES), jnp.float32),
        ],
        input_output_aliases={2 + n: 0} if extra else {},
        compiler_params=pltpu.CompilerParams(vmem_limit_bytes=VMEM_LIMIT),
        cost_estimate=pl.CostEstimate(flops=1024, bytes_accessed=1024, transcendentals=0),
        name="band",
    )(coef, table, *pieces, *extra)


def shards(frames, wavenumbers, band_start, aperture_offset, aperture_count, reference_pixels):
    frame_dev, rows_all, cols_dev = frames.shape
    frame_total = wavenumbers.shape[0]
    n = lax.axis_size("wave")
    me = lax.axis_index("wave")
    rows_dev = rows_all // n
    ncav = band_start.shape[0]
    width_all = cols_dev * lax.axis_size("cols")
    block_cols = cols_dev // aperture_offset.shape[0]
    width = min(256, cols_dev)
    chunks = cols_dev // width
    pos = jnp.stack([me, lax.axis_index("cols") * cols_dev]).astype(jnp.int32)
    pix = reference_pixels[None, :]

    sent, picked = [], 0.0
    for k in range(chunks):
        *parts, part_pick = prep(
            n, rows_dev, k, width, width_all, block_cols, pos, aperture_offset, aperture_count, frames, pix
        )
        sent.append(parts)
        picked = picked + part_pick
        pos, picked = lax.optimization_barrier((pos, picked))

    near = [None] * chunks
    moved = []
    for k in range(chunks):
        parts = sent[k]
        first = parts[1]
        if k >= 1:
            first, _ = lax.optimization_barrier((first, near[k - 1]))
        near[k] = send(first, 1, n)
        far = parts[2:]
        if k >= 2:
            far, _ = lax.optimization_barrier((far, moved[k - 2][2:]))
        moved.append([parts[0], near[k]] + [send(p, 2 + i, n) for i, p in enumerate(far)])

    order = jnp.stack([source(me, s, n) for s in range(n)])
    frame_pos = (order[:, None] * frame_dev + jnp.arange(frame_dev, dtype=jnp.int32)[None, :]).reshape(-1)
    wave_set = jnp.take(wavenumbers.reshape(n, frame_dev), order, axis=0).reshape(-1)
    window = (
        0.5 - 0.5 * jnp.cos(TWO_PI * (frame_pos.astype(jnp.float32) + 0.5) / frame_total)
    ) / math.sqrt(frame_total)
    bins = (band_start[:, None] + jnp.arange(NB, dtype=jnp.int32)[None, :]).astype(jnp.float32)
    angle = bins[:, :, None] * wave_set[None, None, :] * TWO_PI
    table = jnp.stack(
        [jnp.cos(angle) * window, -jnp.sin(angle) * window], axis=1
    ).astype(jnp.bfloat16)

    picked, _ = lax.optimization_barrier((picked, moved[0][2:]))
    middle = table[:, :, NB // 2, :frame_dev].reshape(2 * ncav, frame_dev)
    part = jnp.dot(middle, picked.astype(jnp.bfloat16), preferred_element_type=jnp.float32)
    middle = total_over(total_over(part, "cols"), "wave").reshape(ncav, 2, -1)
    ref = jnp.sum(middle, axis=2)
    power = jnp.sum(middle * middle, axis=(1, 2))
    coef = jnp.transpose(ref / jnp.sqrt(power + EPS)[:, None])

    out = None
    for k in range(chunks):
        out = band(n, k, cols_dev, coef, table, moved[k], out)
    return out


def solution(mesh):
    placed = (
        P("wave", "strips", "cols"),
        P(),
        P(),
        P(("strips", "cols")),
        P(("strips", "cols")),
        P("strips"),
    )
    return jax.shard_map(
        shards,
        mesh=mesh,
        in_specs=placed,
        out_specs=P(None, None, None, ("strips", "wave"), "cols"),
        check_vma=False,
    )
```

time: 217 us -> 123 us (0.57)
  Pallas kernels: 0 us -> 54.5 us
  other arithmetic: 55.6 us -> 16.1 us
  waiting for transfers between devices: 59.4 us -> 21.6 us
  blocking collectives: 33.4 us -> 0 us
  local copies, waits for them, and re-layouts: 38.1 us -> 13.5 us
  matrix products: 20.4 us -> 0.14 us
  starting transfers between devices: 5.97 us -> 15.9 us
  loops' own time: 3.64 us -> 0 us
    all_to_all x1 -> x0, waiting for transfers between devices: 59.4 us -> none  [shards(): lax.all_to_all(masked, 'wave', split_axis=1, concat_axis=0, tiled=True)]
    pallas_call x0 -> x8, Pallas kernels: none -> 54.5 us  [the longest x4 30.3 us: band(): pl.pallas_call(functools.partial(band_kernel, n), out_shape=out, grid=(nc...]
    psum x1 -> x0, blocking collectives: 33.4 us -> none  [shards(): lax.psum((part_re, part_im, part_power), ('wave', 'cols'))]
    dynamic_update_slice x6 -> x0, other arithmetic: 25.6 us -> none  [shards(): lax.map(lambda c: table_block(wavenumbers, band_start, c * 2 * NB, 2 * NB...]
    ppermute x0 -> x16, waiting for transfers between devices: none -> 21.6 us  [the longest x12 17 us: send(): lax.ppermute(value, 'wave', [(i, partner(i, step, n)) for i in range(n)])]
    dot_general x1, matrix products: 20.4 us -> 0.14 us  [shards(): jnp.dot(middle, picked.astype(jnp.bfloat16), preferred_element_type=jnp.f...]
    mul x2 -> x1, other arithmetic: 16 us -> 0.01 us  [shards(): order[:, None] * frame_dev + jnp.arange(frame_dev, dtype=jnp.int32)[None, :]]
    ppermute x0 -> x16, starting transfers between devices: none -> 15.9 us  [the longest x12 8.95 us: send(): lax.ppermute(value, 'wave', [(i, partner(i, step, n)) for i in range(n)])]
  transfers between devices with their start and end apart: 1 -> 16, of which waited for: 1 -> 7; matrix products, arithmetic and copies ran while one was open for 14% -> 14% of each run, Pallas kernels for 0% -> 33%
where the time goes in v1:
time: 123 us; the launch traced here: 122 us
  Pallas kernels  54.5 us (44%)
  waiting for transfers between devices  21.6 us (18%)
  other arithmetic  16.1 us (13%)
  starting transfers between devices  15.9 us (13%)
  local copies, waits for them, and re-layouts  13.5 us (11%)
    pallas_call x4, Pallas kernels, band(): pl.pallas_call(functools.partial(band_kernel, n), out_shape=out, grid=(nc...  30.3 us
    pallas_call x4, Pallas kernels, prep(): pl.pallas_call(functools.partial(prep_kernel, n, rows_dev, chunk, width_a...  24.2 us
    ppermute x12, waiting for transfers between devices, send(): lax.ppermute(value, 'wave', [(i, partner(i, step, n)) for i in range(n)])  17 us
    unnamed x60, local copies, waits for them, and re-layouts  12.7 us
    another operation x1, other arithmetic  12.3 us
    ppermute x12, starting transfers between devices, send(): lax.ppermute(value, 'wave', [(i, partner(i, step, n)) for i in range(n)])  8.95 us
    ppermute x4, starting transfers between devices, total_over(): value = value + lax.ppermute(value, axis, [(i, i ^ step) for i in range(n)])  6.94 us
    ppermute x4, waiting for transfers between devices, total_over(): value = value + lax.ppermute(value, axis, [(i, i ^ step) for i in range(n)])  4.61 us
  transfers between devices with their start and end apart: 16, of which 7 were waited for; matrix products, arithmetic and copies ran while one was open for 14% of the time, Pallas kernels for 33%

profile of v1, /device:TPU:0, one launch (start us, length us, event | category | flops | bytes accessed | tf_op | source)
XLA Modules:
  0.0 121.9 jit_solution(14579280772426325898)
XLA Ops:
  2.1 5.8 %prep.4 = (bf16[4,256,256]{2,1,0:T(8,128)(2,1)S(1)}, bf16[4,256,256]{2,1,0:T(8,128)(2,1)}, bf16[4,256,256]{2,1,0:T(8,128)(2,1)S(1)}, bf16[4,256,256]{2,1,0:T(8,128)(2,1)S(1)}, f32[256,256]{1,0:T(8,128)S(1)}) custom-call(s32[2]{0:T(128)S(1)} %pad_add_fusion.1.pos_ref, s32[8]{0:T(128)S(1)} %copy-done.18, s32[8]{0:T(128)S(1)} %copy-done.20, ...), custom_call_target="tpu_custom_call" | custom-call | flops 1024 | bytes 1024 | tf_op jit(solution)/shard_map/prep/pallas_call | solution.py:79
  8.7 2.9 %collective-permute-start = (bf16[4,256,256]{2,1,0:T(8,128)(2,1)S(1)}, bf16[4,256,256]{2,1,0:T(8,128)(2,1)S(1)}, u32[]{:S(2)}, u32[]{:S(2)}) collective-permute-start(bf16[4,256,256]{2,1,0:T(8,128)(2,1)S(1)} %get-tuple-element.51), channel_id=1, source_target_pairs={{0,8},{4,12},{8,0},{12,4},{1,9},{5,13},{9,1},{13,5},{2,10},{6,14},... | collective-permute-start | bytes 1572872 | tf_op jit(solution)/shard_map/ppermute | solution.py:31
  11.8 5.8 %prep.5 = (bf16[4,256,256]{2,1,0:T(8,128)(2,1)S(1)}, bf16[4,256,256]{2,1,0:T(8,128)(2,1)S(1)}, bf16[4,256,256]{2,1,0:T(8,128)(2,1)}, bf16[4,256,256]{2,1,0:T(8,128)(2,1)}, f32[256,256]{1,0:T(8,128)S(1)}) custom-call(s32[2]{0:T(128)S(1)} %pad_add_fusion.1.pos_ref, s32[8]{0:T(128)S(1)} %copy-done.18, s32[8]{0:T(128)S(1)} %copy-done.20, ...), custom_call_target="tpu_custom_call" | custom-call | flops 1024 | bytes 1024 | tf_op jit(solution)/shard_map/prep/pallas_call | solution.py:79
  19.2 2.0 %collective-permute-start.10 = (bf16[4,256,256]{2,1,0:T(8,128)(2,1)}, bf16[4,256,256]{2,1,0:T(8,128)(2,1)}, u32[]{:S(2)}, u32[]{:S(2)}) collective-permute-start(bf16[4,256,256]{2,1,0:T(8,128)(2,1)} %get-tuple-element.64), channel_id=1, source_target_pairs={{0,8},{4,12},{8,0},{12,4},{1,9},{5,13},{9,1},{13,5},{2,10},{6,14},... | collective-permute-start | bytes 1572872 | tf_op jit(solution)/shard_map/ppermute | solution.py:31
  22.0 6.0 %prep.6 = (bf16[4,256,256]{2,1,0:T(8,128)(2,1)S(1)}, bf16[4,256,256]{2,1,0:T(8,128)(2,1)}, bf16[4,256,256]{2,1,0:T(8,128)(2,1)}, bf16[4,256,256]{2,1,0:T(8,128)(2,1)}, f32[256,256]{1,0:T(8,128)S(1)}) custom-call(s32[2]{0:T(128)S(1)} %pad_add_fusion.1.pos_ref, s32[8]{0:T(128)S(1)} %copy-done.19, s32[8]{0:T(128)S(1)} %copy-done.21, ...), custom_call_target="tpu_custom_call" | custom-call | flops 1024 | bytes 1024 | tf_op jit(solution)/shard_map/prep/pallas_call | solution.py:79
  28.0 0.8 copy-done.2
  29.1 0.8 copy-done.14
  30.9 1.0 collective-permute-done.7.rest_1_
  32.0 12.3 %multiply_convert_fusion.1 = (bf16[6,1,128,1024]{3,2,1,0:T(8,128)(2,1)S(1)}, bf16[6,1,128,1024]{3,2,1,0:T(8,128)(2,1)S(1)}) fusion(f32[1024]{0:T(1024)S(1)} %bitcast.26, f32[1024]{0:T(1024)S(1)} %bitcast.27, f32[6,128]{1,0:T(8,128)S(1)} %add_convert_fusion), kind=kLoop, calls=%fused_computation.5 | loop fusion | flops 5505024 | bytes 3156992 | tf_op jit(solution)/shard_map/convert
  44.4 6.5 %prep.7 = (bf16[4,256,256]{2,1,0:T(8,128)(2,1)S(1)}, bf16[4,256,256]{2,1,0:T(8,128)(2,1)}, bf16[4,256,256]{2,1,0:T(8,128)(2,1)}, bf16[4,256,256]{2,1,0:T(8,128)(2,1)}, f32[256,256]{1,0:T(8,128)S(1)}) custom-call(s32[2]{0:T(128)S(1)} %pad_add_fusion.1.pos_ref, s32[8]{0:T(128)S(1)} %copy-done.19, s32[8]{0:T(128)S(1)} %copy-done.21, ...), custom_call_target="tpu_custom_call" | custom-call | flops 1024 | bytes 1024 | tf_op jit(solution)/shard_map/prep/pallas_call | solution.py:79
  51.0 0.8 copy-done.6
  53.6 2.1 %collective-permute-start.2 = (f32[12,256]{1,0:T(8,128)S(1)}, f32[12,256]{1,0:T(8,128)S(1)}, u32[]{:S(2)}, u32[]{:S(2)}) collective-permute-start(f32[12,256]{1,0:T(8,128)S(1)} %fusion.5), channel_id=1, source_target_pairs={{0,1},{1,0},{2,3},{3,2},{4,5},{5,4},{6,7},{7,6},{8,9},{9,8},{10,11... | collective-permute-start | bytes 36872 | tf_op jit(solution)/shard_map/ppermute | solution.py:40
  55.7 1.7 %collective-permute-done.2 = f32[12,256]{1,0:T(8,128)S(1)} collective-permute-done((f32[12,256]{1,0:T(8,128)S(1)}, f32[12,256]{1,0:T(8,128)S(1)}, u32[]{:S(2)}, u32[]{:S(2)}) %collective-permute-start.2) | collective-permute-done | bytes 12320 | tf_op jit(solution)/shard_map/ppermute | solution.py:40
  57.4 3.0 %collective-permute-start.3 = (f32[12,256]{1,0:T(8,128)S(1)}, f32[12,256]{1,0:T(8,128)S(1)}, u32[]{:S(2)}, u32[]{:S(2)}) collective-permute-start(f32[12,256]{1,0:T(8,128)S(1)} %add.99), channel_id=1, source_target_pairs={{0,2},{1,3},{2,0},{3,1},{4,6},{5,7},{6,4},{7,5},{8,10},{9,11},{10,... | collective-permute-start | bytes 36872 | tf_op jit(solution)/shard_map/ppermute | solution.py:40
  60.5 1.7 %collective-permute-done.3 = f32[12,256]{1,0:T(8,128)S(1)} collective-permute-done((f32[12,256]{1,0:T(8,128)S(1)}, f32[12,256]{1,0:T(8,128)S(1)}, u32[]{:S(2)}, u32[]{:S(2)}) %collective-permute-start.3) | collective-permute-done | bytes 12320 | tf_op jit(solution)/shard_map/ppermute | solution.py:40
  62.2 1.2 collective-permute-done.4
  63.4 1.8 %collective-permute-start.5 = (f32[12,256]{1,0:T(8,128)S(1)}, f32[12,256]{1,0:T(8,128)S(1)}, u32[]{:S(2)}, u32[]{:S(2)}) collective-permute-start(f32[12,256]{1,0:T(8,128)S(1)} %add.101), channel_id=1, source_target_pairs={{0,8},{4,12},{8,0},{12,4},{1,9},{5,13},{9,1},{13,5},{2,10},{6,14},... | collective-permute-start | bytes 36872 | tf_op jit(solution)/shard_map/ppermute | solution.py:40
  65.2 2.2 %pad_maximum_fusion.table_ref = bf16[6,2,128,1024]{3,2,1,0:T(8,128)(2,1)S(1)} fusion(bf16[6,1,128,1024]{3,2,1,0:T(8,128)(2,1)} %copy-done.25, bf16[6,1,128,1024]{3,2,1,0:T(8,128)(2,1)} %copy-done.24), kind=kLoop, calls=%fused_computation.2 | loop fusion | flops 1572864 | bytes 6291456 | tf_op jit(solution)/shard_map/stack | solution.py:198
  67.7 1.0 collective-permute-start.15
  68.7 0.9 collective-permute-start.12
  69.6 1.4 %collective-permute-start.13 = (bf16[4,256,256]{2,1,0:T(8,128)(2,1)}, bf16[4,256,256]{2,1,0:T(8,128)(2,1)}, u32[]{:S(2)}, u32[]{:S(2)}) collective-permute-start(bf16[4,256,256]{2,1,0:T(8,128)(2,1)} %get-tuple-element.67), channel_id=1, source_target_pairs={{0,12},{4,8},{8,4},{12,0},{1,13},{5,9},{9,5},{13,1},{2,14},{6,10},... | collective-permute-start | bytes 1572872 | tf_op jit(solution)/shard_map/ppermute | solution.py:31
  71.5 1.0 copy-done.9
  72.5 1.0 copy-done.11
  73.6 1.0 copy-done.13
  74.6 1.0 copy-done.15
  75.7 6.9 %band.4.rest_4_ = bf16[6,2,128,4,1024]{4,3,2,1,0:T(4,128)(2,1)} custom-call(f32[2,6]{1,0:T(2,128)S(1)} %divide_bitcast_fusion.coef_ref, bf16[6,2,128,1024]{3,2,1,0:T(8,128)(2,1)S(1)} %pad_maximum_fusion.table_ref, bf16[4,256,256]{2,1,0:T(8,128)(2,1)S(1)} %copy-done.9, bf16[4,256,256]{2,1,0:T(8,128)(2,1)S(1)} %copy-done.15, ...), custom_call_target="tpu_custom_call" | custom-call | flops 1024 | bytes 1024 | tf_op jit(solution)/shard_map/band/pallas_call | solution.py:132
  82.6 7.7 %band.5.rest_4_ = bf16[6,2,128,4,1024]{4,3,2,1,0:T(4,128)(2,1)} custom-call(f32[2,6]{1,0:T(2,128)S(1)} %divide_bitcast_fusion.coef_ref, bf16[6,2,128,1024]{3,2,1,0:T(8,128)(2,1)S(1)} %pad_maximum_fusion.table_ref, bf16[4,256,256]{2,1,0:T(8,128)(2,1)S(1)} %copy-done.1, bf16[4,256,256]{2,1,0:T(8,128)(2,1)S(1)} %copy-done.5, ...), custom_call_target="tpu_custom_call", output_to_operand_aliasing={{}: (6, {})} | custom-call | flops 1024 | bytes 1024 | tf_op jit(solution)/shard_map/band/pallas_call | solution.py:132
  90.3 1.3 %collective-permute-done.15.rest_3_ = bf16[4,256,256]{2,1,0:T(8,128)(2,1)} collective-permute-done((bf16[4,256,256]{2,1,0:T(8,128)(2,1)}, bf16[4,256,256]{2,1,0:T(8,128)(2,1)}, u32[]{:S(2)}, u32[]{:S(2)}) %collective-permute-start.15) | collective-permute-done | bytes 524320 | tf_op jit(solution)/shard_map/ppermute | solution.py:31
  91.6 7.9 %band.6.rest_4_ = bf16[6,2,128,4,1024]{4,3,2,1,0:T(4,128)(2,1)} custom-call(f32[2,6]{1,0:T(2,128)S(1)} %divide_bitcast_fusion.coef_ref, bf16[6,2,128,1024]{3,2,1,0:T(8,128)(2,1)S(1)} %pad_maximum_fusion.table_ref, bf16[4,256,256]{2,1,0:T(8,128)(2,1)S(1)} %copy-done.3, ...), custom_call_target="tpu_custom_call", output_to_operand_aliasing={{}: (6, {})} | custom-call | flops 1024 | bytes 1024 | tf_op jit(solution)/shard_map/band/pallas_call | solution.py:132
  99.5 5.6 %collective-permute-done.12.rest_2_ = bf16[4,256,256]{2,1,0:T(8,128)(2,1)} collective-permute-done((bf16[4,256,256]{2,1,0:T(8,128)(2,1)}, bf16[4,256,256]{2,1,0:T(8,128)(2,1)}, u32[]{:S(2)}, u32[]{:S(2)}) %collective-permute-start.12) | collective-permute-done | bytes 524320 | tf_op jit(solution)/shard_map/ppermute | solution.py:31
  105.0 9.0 %collective-permute-done.13.rest_3_ = bf16[4,256,256]{2,1,0:T(8,128)(2,1)} collective-permute-done((bf16[4,256,256]{2,1,0:T(8,128)(2,1)}, bf16[4,256,256]{2,1,0:T(8,128)(2,1)}, u32[]{:S(2)}, u32[]{:S(2)}) %collective-permute-start.13) | collective-permute-done | bytes 524320 | tf_op jit(solution)/shard_map/ppermute | solution.py:31
  114.1 7.8 %band.7 = bf16[6,2,128,4,1024]{4,3,2,1,0:T(4,128)(2,1)} custom-call(f32[2,6]{1,0:T(2,128)S(1)} %divide_bitcast_fusion.coef_ref, bf16[6,2,128,1024]{3,2,1,0:T(8,128)(2,1)S(1)} %pad_maximum_fusion.table_ref, bf16[4,256,256]{2,1,0:T(8,128)(2,1)S(1)} %copy-done.7, bf16[4,256,256]{2,1,0:T(8,128)(2,1)} %collective-permute-done.9.rest_1_, ...), custom_call_target="tpu_custom_call", output_to_operand_aliasing={{}: (6, {})} | custom-call | flops 1024 | bytes 1024 | tf_op jit(solution)/shard_map/band/pallas_call | solution.py:132
  (96 shorter events, 9.4 us)
Async XLA Ops:
  8.7 43.2 %collective-permute-start = (bf16[4,256,256]{2,1,0:T(8,128)(2,1)S(1)}, bf16[4,256,256]{2,1,0:T(8,128)(2,1)S(1)}, u32[]{:S(2)}, u32[]{:S(2)}) collective-permute-start(bf16[4,256,256]{2,1,0:T(8,128)(2,1)S(1)} %get-tuple-element.51), channel_id=1, source_target_pairs={{0,8},{4,12},{8,0},{12,4},{1,9},{5,13},{9,1},{13,5},{2,10},{6,14},... | collective-permute-start | bytes 1572872 | tf_op jit(solution)/shard_map/ppermute | solution.py:31
  11.6 41.1 %collective-permute-start.1 = (bf16[4,256,256]{2,1,0:T(8,128)(2,1)S(1)}, bf16[4,256,256]{2,1,0:T(8,128)(2,1)S(1)}, u32[]{:S(2)}, u32[]{:S(2)}) collective-permute-start(bf16[4,256,256]{2,1,0:T(8,128)(2,1)S(1)} %get-tuple-element.52), channel_id=1, source_target_pairs={{0,12},{4,8},{8,4},{12,0},{1,13},{5,9},{9,5},{13,1},{2,14},{6,10},... | collective-permute-start | bytes 1572872 | tf_op jit(solution)/shard_map/ppermute | solution.py:31
  11.6 17.5 %collective-permute-start.6 = (bf16[4,256,256]{2,1,0:T(8,128)(2,1)}, bf16[4,256,256]{2,1,0:T(8,128)(2,1)S(1)}, u32[]{:S(2)}, u32[]{:S(2)}) collective-permute-start(bf16[4,256,256]{2,1,0:T(8,128)(2,1)} %get-tuple-element.58), channel_id=1, source_target_pairs={{0,4},{4,0},{8,12},{12,8},{1,5},{5,1},{9,13},{13,9},{2,6},{6,2},{1... | collective-permute-start | bytes 1572872 | tf_op jit(solution)/shard_map/ppermute | solution.py:31
  11.8 10.2 %copy-start.17 = (s32[256]{0:T(256)S(1)}, s32[256]{0:T(256)}, u32[]{:S(2)}) copy-start(s32[256]{0:T(256)} %param.11) | copy-start | bytes 3076
  11.8 10.2 %copy-start.19 = (s32[8]{0:T(128)S(1)}, s32[8]{0:T(128)}, u32[]{:S(2)}) copy-start(s32[8]{0:T(128)} %off_ref.7) | copy-start | bytes 100
  11.8 10.2 %copy-start.21 = (s32[8]{0:T(128)S(1)}, s32[8]{0:T(128)}, u32[]{:S(2)}) copy-start(s32[8]{0:T(128)} %cnt_ref.7) | copy-start | bytes 100
  19.2 48.5 %collective-permute-start.10 = (bf16[4,256,256]{2,1,0:T(8,128)(2,1)}, bf16[4,256,256]{2,1,0:T(8,128)(2,1)}, u32[]{:S(2)}, u32[]{:S(2)}) collective-permute-start(bf16[4,256,256]{2,1,0:T(8,128)(2,1)} %get-tuple-element.64), channel_id=1, source_target_pairs={{0,8},{4,12},{8,0},{12,4},{1,9},{5,13},{9,1},{13,5},{2,10},{6,14},... | collective-permute-start | bytes 1572872 | tf_op jit(solution)/shard_map/ppermute | solution.py:31
  21.2 47.5 %collective-permute-start.11 = (bf16[4,256,256]{2,1,0:T(8,128)(2,1)}, bf16[4,256,256]{2,1,0:T(8,128)(2,1)}, u32[]{:S(2)}, u32[]{:S(2)}) collective-permute-start(bf16[4,256,256]{2,1,0:T(8,128)(2,1)} %get-tuple-element.65), channel_id=1, source_target_pairs={{0,12},{4,8},{8,4},{12,0},{1,13},{5,9},{9,5},{13,1},{2,14},{6,10},... | collective-permute-start | bytes 1572872 | tf_op jit(solution)/shard_map/ppermute | solution.py:31
  21.9 7.1 %copy-start.27 = (f32[1024]{0:T(1024)S(1)}, f32[1024]{0:T(1024)}, u32[]{:S(2)}) copy-start(f32[1024]{0:T(1024)} %param.7) | copy-start | bytes 12292
  21.9 8.0 %copy-start.23 = (bf16[4,256,256]{2,1,0:T(8,128)(2,1)S(1)}, bf16[4,256,256]{2,1,0:T(8,128)(2,1)}, u32[]{:S(2)}) copy-start(bf16[4,256,256]{2,1,0:T(8,128)(2,1)} %copy-done.22) | copy-start | bytes 1572868
  22.0 8.8 %copy-start.28 = (s32[6]{0:T(128)S(1)}, s32[6]{0:T(128)}, u32[]{:S(2)}) copy-start(s32[6]{0:T(128)} %param.8) | copy-start | bytes 76
  30.0 1.9 %collective-permute-start.7 = (bf16[4,256,256]{2,1,0:T(8,128)(2,1)S(1)}, bf16[4,256,256]{2,1,0:T(8,128)(2,1)S(1)}, u32[]{:S(2)}, u32[]{:S(2)}) collective-permute-start(bf16[4,256,256]{2,1,0:T(8,128)(2,1)S(1)} %copy-done.23), channel_id=1, source_target_pairs={{0,4},{4,0},{8,12},{12,8},{1,5},{5,1},{9,13},{13,9},{2,6},{6,2},{1... | collective-permute-start | bytes 1572872 | tf_op jit(solution)/shard_map/ppermute | solution.py:31
  30.7 13.7 %copy-start.26 = (f32[256,256]{1,0:T(8,128)S(1)}, f32[256,256]{1,0:T(8,128)}, u32[]{:S(2)}) copy-start(f32[256,256]{1,0:T(8,128)} %add.96) | copy-start | bytes 786436
  31.9 19.1 %copy-start.4 = (bf16[4,256,256]{2,1,0:T(8,128)(2,1)}, bf16[4,256,256]{2,1,0:T(8,128)(2,1)S(1)}, u32[]{:S(2)}) copy-start(bf16[4,256,256]{2,1,0:T(8,128)(2,1)S(1)} %collective-permute-done.7.rest_1_) | copy-start | bytes 1572868
  31.9 37.7 %collective-permute-start.8 = (bf16[4,256,256]{2,1,0:T(8,128)(2,1)}, bf16[4,256,256]{2,1,0:T(8,128)(2,1)}, u32[]{:S(2)}, u32[]{:S(2)}) collective-permute-start(bf16[4,256,256]{2,1,0:T(8,128)(2,1)} %get-tuple-element.60), channel_id=1, source_target_pairs={{0,4},{4,0},{8,12},{12,8},{1,5},{5,1},{9,13},{13,9},{2,6},{6,2},{1... | collective-permute-start | bytes 1572872 | tf_op jit(solution)/shard_map/ppermute | solution.py:31
  44.4 7.5 %copy-start.24 = (bf16[6,1,128,1024]{3,2,1,0:T(8,128)(2,1)}, bf16[6,1,128,1024]{3,2,1,0:T(8,128)(2,1)S(1)}, u32[]{:S(2)}) copy-start(bf16[6,1,128,1024]{3,2,1,0:T(8,128)(2,1)S(1)} %get-tuple-element.79) | copy-start | bytes 4718596
  44.4 7.5 %copy-start.25 = (bf16[6,1,128,1024]{3,2,1,0:T(8,128)(2,1)}, bf16[6,1,128,1024]{3,2,1,0:T(8,128)(2,1)S(1)}, u32[]{:S(2)}) copy-start(bf16[6,1,128,1024]{3,2,1,0:T(8,128)(2,1)S(1)} %get-tuple-element.80) | copy-start | bytes 4718596
  53.6 3.8 %collective-permute-start.2 = (f32[12,256]{1,0:T(8,128)S(1)}, f32[12,256]{1,0:T(8,128)S(1)}, u32[]{:S(2)}, u32[]{:S(2)}) collective-permute-start(f32[12,256]{1,0:T(8,128)S(1)} %fusion.5), channel_id=1, source_target_pairs={{0,1},{1,0},{2,3},{3,2},{4,5},{5,4},{6,7},{7,6},{8,9},{9,8},{10,11... | collective-permute-start | bytes 36872 | tf_op jit(solution)/shard_map/ppermute | solution.py:40
  57.4 4.8 %collective-permute-start.3 = (f32[12,256]{1,0:T(8,128)S(1)}, f32[12,256]{1,0:T(8,128)S(1)}, u32[]{:S(2)}, u32[]{:S(2)}) collective-permute-start(f32[12,256]{1,0:T(8,128)S(1)} %add.99), channel_id=1, source_target_pairs={{0,2},{1,3},{2,0},{3,1},{4,6},{5,7},{6,4},{7,5},{8,10},{9,11},{10,... | collective-permute-start | bytes 36872 | tf_op jit(solution)/shard_map/ppermute | solution.py:40
  62.2 1.2 collective-permute-start.4
  63.4 7.6 %collective-permute-start.5 = (f32[12,256]{1,0:T(8,128)S(1)}, f32[12,256]{1,0:T(8,128)S(1)}, u32[]{:S(2)}, u32[]{:S(2)}) collective-permute-start(f32[12,256]{1,0:T(8,128)S(1)} %add.101), channel_id=1, source_target_pairs={{0,8},{4,12},{8,0},{12,4},{1,9},{5,13},{9,1},{13,5},{2,10},{6,14},... | collective-permute-start | bytes 36872 | tf_op jit(solution)/shard_map/ppermute | solution.py:40
  67.4 22.9 %collective-permute-start.14 = (bf16[4,256,256]{2,1,0:T(8,128)(2,1)}, bf16[4,256,256]{2,1,0:T(8,128)(2,1)}, u32[]{:S(2)}, u32[]{:S(2)}) collective-permute-start(bf16[4,256,256]{2,1,0:T(8,128)(2,1)} %get-tuple-element.71), channel_id=1, source_target_pairs={{0,8},{4,12},{8,0},{12,4},{1,9},{5,13},{9,1},{13,5},{2,10},{6,14},... | collective-permute-start | bytes 1572872 | tf_op jit(solution)/shard_map/ppermute | solution.py:31
  67.7 24.0 %collective-permute-start.15 = (bf16[4,256,256]{2,1,0:T(8,128)(2,1)}, bf16[4,256,256]{2,1,0:T(8,128)(2,1)}, u32[]{:S(2)}, u32[]{:S(2)}) collective-permute-start(bf16[4,256,256]{2,1,0:T(8,128)(2,1)} %get-tuple-element.72), channel_id=1, source_target_pairs={{0,12},{4,8},{8,4},{12,0},{1,13},{5,9},{9,5},{13,1},{2,14},{6,10},... | collective-permute-start | bytes 1572872 | tf_op jit(solution)/shard_map/ppermute | solution.py:31
  68.7 36.3 %collective-permute-start.12 = (bf16[4,256,256]{2,1,0:T(8,128)(2,1)}, bf16[4,256,256]{2,1,0:T(8,128)(2,1)}, u32[]{:S(2)}, u32[]{:S(2)}) collective-permute-start(bf16[4,256,256]{2,1,0:T(8,128)(2,1)} %get-tuple-element.66), channel_id=1, source_target_pairs={{0,8},{4,12},{8,0},{12,4},{1,9},{5,13},{9,1},{13,5},{2,10},{6,14},... | collective-permute-start | bytes 1572872 | tf_op jit(solution)/shard_map/ppermute | solution.py:31
  69.6 44.5 %collective-permute-start.13 = (bf16[4,256,256]{2,1,0:T(8,128)(2,1)}, bf16[4,256,256]{2,1,0:T(8,128)(2,1)}, u32[]{:S(2)}, u32[]{:S(2)}) collective-permute-start(bf16[4,256,256]{2,1,0:T(8,128)(2,1)} %get-tuple-element.67), channel_id=1, source_target_pairs={{0,12},{4,8},{8,4},{12,0},{1,13},{5,9},{9,5},{13,1},{2,14},{6,10},... | collective-permute-start | bytes 1572872 | tf_op jit(solution)/shard_map/ppermute | solution.py:31
  71.0 43.1 %collective-permute-start.9 = (bf16[4,256,256]{2,1,0:T(8,128)(2,1)}, bf16[4,256,256]{2,1,0:T(8,128)(2,1)}, u32[]{:S(2)}, u32[]{:S(2)}) collective-permute-start(bf16[4,256,256]{2,1,0:T(8,128)(2,1)} %get-tuple-element.61), channel_id=1, source_target_pairs={{0,4},{4,0},{8,12},{12,8},{1,5},{5,1},{9,13},{13,9},{2,6},{6,2},{1... | collective-permute-start | bytes 1572872 | tf_op jit(solution)/shard_map/ppermute | solution.py:31
  71.5 1.1 copy-start.9
  72.5 1.0 copy-start.11
  75.7 6.9 %copy-start.1 = (bf16[4,256,256]{2,1,0:T(8,128)(2,1)S(1)}, bf16[4,256,256]{2,1,0:T(8,128)(2,1)}, u32[]{:S(2)}) copy-start(bf16[4,256,256]{2,1,0:T(8,128)(2,1)} %copy-done) | copy-start | bytes 1572868
  75.7 6.9 %copy-start.5 = (bf16[4,256,256]{2,1,0:T(8,128)(2,1)S(1)}, bf16[4,256,256]{2,1,0:T(8,128)(2,1)}, u32[]{:S(2)}) copy-start(bf16[4,256,256]{2,1,0:T(8,128)(2,1)} %copy-done.4) | copy-start | bytes 1572868
  82.6 9.0 %copy-start.3 = (bf16[4,256,256]{2,1,0:T(8,128)(2,1)S(1)}, bf16[4,256,256]{2,1,0:T(8,128)(2,1)}, u32[]{:S(2)}) copy-start(bf16[4,256,256]{2,1,0:T(8,128)(2,1)} %copy-done.2) | copy-start | bytes 1572868
  91.6 22.5 %copy-start.7 = (bf16[4,256,256]{2,1,0:T(8,128)(2,1)S(1)}, bf16[4,256,256]{2,1,0:T(8,128)(2,1)}, u32[]{:S(2)}) copy-start(bf16[4,256,256]{2,1,0:T(8,128)(2,1)} %copy-done.6) | copy-start | bytes 1572868
  (13 other events, 10.5 us)

commit v2 on v1

--- a/solution.py
+++ b/solution.py
@@ -25,6 +25,12 @@
     if n & (n - 1) == 0:
         return me ^ step
     return (me + n - step) % n
+
+
+def column_cuts(cols_dev):
+    if cols_dev % 256 or cols_dev < 512:
+        return [(LANES, i) for i in range(cols_dev // LANES)]
+    return [(128, 0)] + [(256, i) for i in range(1, cols_dev // 256)] + [(128, 1)]
 
 
 def send(value, step, n):
@@ -106,18 +112,23 @@
     def _():
         for r in range(rows_dev):
             for i in range(n):
-                flat[r, i * frame_dev:(i + 1) * frame_dev, :] = pieces[i][r]
+                flat[i * frame_dev:(i + 1) * frame_dev, r * width:(r + 1) * width] = pieces[i][r]
 
     ca = coef_ref[0, cav]
     cb = coef_ref[1, cav]
-    for r in range(rows_dev):
-        table = table_ref[0].reshape(2 * nb, table_ref.shape[3])
-        spec = jnp.dot(table, flat[r], preferred_element_type=jnp.float32)
+    table = table_ref[0].reshape(2 * nb, table_ref.shape[3])
+    group = min(rows_dev, max(1, 256 // width))
+    for g in range(0, rows_dev, group):
+        spec = jnp.dot(
+            table, flat[:, g * width:(g + group) * width], preferred_element_type=jnp.float32
+        )
         re, im = spec[:nb], spec[nb:]
         both = (re * ca + im * cb, im * ca - re * cb)
-        for b in range(width // LANES):
-            for q in range(2):
-                mixed[q, b, pl.ds(r, nb, stride=rows_dev), :] = both[q][:, b * LANES:(b + 1) * LANES]
+        for r in range(group):
+            for b in range(width // LANES):
+                first = r * width + b * LANES
+                for q in range(2):
+                    mixed[q, b, pl.ds(g + r, nb, stride=rows_dev), :] = both[q][:, first:first + LANES]
     for b in range(width // LANES):
         for q in range(2):
             value = mixed[q, b].reshape(nb, rows_dev, LANES).astype(jnp.bfloat16)
@@ -141,7 +152,7 @@
         + [pl.BlockSpec(memory_space=pl.ANY)] * len(extra),
         out_specs=pl.BlockSpec((1, 2, nb, rows_dev, width), lambda c: (c, 0, 0, 0, chunk)),
         scratch_shapes=[
-            pltpu.VMEM((rows_dev, frame_total, width), jnp.bfloat16),
+            pltpu.VMEM((frame_total, rows_dev * width), jnp.bfloat16),
             pltpu.VMEM((2, width // LANES, nb * rows_dev, LANES), jnp.float32),
         ],
         input_output_aliases={2 + n: 0} if extra else {},
@@ -160,15 +171,15 @@
     ncav = band_start.shape[0]
     width_all = cols_dev * lax.axis_size("cols")
     block_cols = cols_dev // aperture_offset.shape[0]
-    width = min(256, cols_dev)
-    chunks = cols_dev // width
+    cuts = column_cuts(cols_dev)
+    chunks = len(cuts)
     pos = jnp.stack([me, lax.axis_index("cols") * cols_dev]).astype(jnp.int32)
     pix = reference_pixels[None, :]
 
     sent, picked = [], 0.0
-    for k in range(chunks):
+    for width, index in cuts:
         *parts, part_pick = prep(
-            n, rows_dev, k, width, width_all, block_cols, pos, aperture_offset, aperture_count, frames, pix
+            n, rows_dev, index, width, width_all, block_cols, pos, aperture_offset, aperture_count, frames, pix
         )
         sent.append(parts)
         picked = picked + part_pick
@@ -184,7 +195,7 @@
         near[k] = send(first, 1, n)
         far = parts[2:]
         if k >= 2:
-            far, _ = lax.optimization_barrier((far, moved[k - 2][2:]))
+            far = [lax.optimization_barrier((p, q))[0] for p, q in zip(far, moved[k - 2][2:])]
         moved.append([parts[0], near[k]] + [send(p, 2 + i, n) for i, p in enumerate(far)])
 
     order = jnp.stack([source(me, s, n) for s in range(n)])
@@ -199,7 +210,7 @@
         [jnp.cos(angle) * window, -jnp.sin(angle) * window], axis=1
     ).astype(jnp.bfloat16)
 
-    picked, _ = lax.optimization_barrier((picked, moved[0][2:]))
+    picked, _ = lax.optimization_barrier((picked, moved[min(1, chunks - 1)][2:]))
     middle = table[:, :, NB // 2, :frame_dev].reshape(2 * ncav, frame_dev)
     part = jnp.dot(middle, picked.astype(jnp.bfloat16), preferred_element_type=jnp.float32)
     middle = total_over(total_over(part, "cols"), "wave").reshape(ncav, 2, -1)
@@ -209,7 +220,7 @@
 
     out = None
     for k in range(chunks):
-        out = band(n, k, cols_dev, coef, table, moved[k], out)
+        out = band(n, cuts[k][1], cols_dev, coef, table, moved[k], out)
     return out
 
 

time: 123 us -> 126 us (1.024)
  waiting for transfers between devices: 21.6 us -> 13.6 us
  local copies, waits for them, and re-layouts: 13.5 us -> 18.4 us
  Pallas kernels: 54.5 us -> 58.8 us
  starting transfers between devices: 15.9 us -> 17.2 us
  other arithmetic: 16.1 us -> 17.4 us
    ppermute x12 -> x15, waiting for transfers between devices: 17 us -> 0.04 us  [send(): lax.ppermute(value, 'wave', [(i, partner(i, step, n)) for i in range(n)])]
    ppermute x4, waiting for transfers between devices: 4.61 us -> 13.5 us  [total_over(): value = value + lax.ppermute(value, axis, [(i, i ^ step) for i in range(n)])]
    unnamed x60 -> x70, local copies, waits for them, and re-layouts: 12.7 us -> 16.9 us
    pallas_call x4 -> x5, Pallas kernels: 30.3 us -> 33.7 us  [band(): pl.pallas_call(functools.partial(band_kernel, n), out_shape=out, grid=(nc...]
    ppermute x12 -> x15, starting transfers between devices: 8.95 us -> 11.1 us  [send(): lax.ppermute(value, 'wave', [(i, partner(i, step, n)) for i in range(n)])]
    pallas_call x4 -> x5, Pallas kernels: 24.2 us -> 25.1 us  [prep(): pl.pallas_call(functools.partial(prep_kernel, n, rows_dev, chunk, width_a...]
  transfers between devices with their start and end apart: 16 -> 19, of which waited for: 7 -> 4; matrix products, arithmetic and copies ran while one was open for 14% -> 16% of each run, Pallas kernels for 33% -> 39%
where the time goes in v2:
time: 126 us
  Pallas kernels  58.8 us (47%)
  local copies, waits for them, and re-layouts  18.4 us (15%)
  other arithmetic  17.4 us (14%)
  starting transfers between devices  17.2 us (14%)
  waiting for transfers between devices  13.6 us (11%)
    pallas_call x5, Pallas kernels, band(): pl.pallas_call(functools.partial(band_kernel, n), out_shape=out, grid=(nc...  33.7 us
    pallas_call x5, Pallas kernels, prep(): pl.pallas_call(functools.partial(prep_kernel, n, rows_dev, chunk, width_a...  25.1 us
    unnamed x70, local copies, waits for them, and re-layouts  16.9 us
    ppermute x4, waiting for transfers between devices, total_over(): value = value + lax.ppermute(value, axis, [(i, i ^ step) for i in range(n)])  13.5 us
    another operation x1, other arithmetic  13 us
    ppermute x15, starting transfers between devices, send(): lax.ppermute(value, 'wave', [(i, partner(i, step, n)) for i in range(n)])  11.1 us
    ppermute x4, starting transfers between devices, total_over(): value = value + lax.ppermute(value, axis, [(i, i ^ step) for i in range(n)])  6.12 us
  transfers between devices with their start and end apart: 19, of which 4 were waited for; matrix products, arithmetic and copies ran while one was open for 16% of the time, Pallas kernels for 39%

profile of v2, /device:TPU:0, one launch (start us, length us, event | category | flops | bytes accessed | tf_op | source)
XLA Modules:
  0.0 125.8 jit_solution(10979748443611760909)
XLA Ops:
  2.1 3.9 %prep.5 = (bf16[4,256,128]{2,1,0:T(8,128)(2,1)S(1)}, bf16[4,256,128]{2,1,0:T(8,128)(2,1)S(1)}, bf16[4,256,128]{2,1,0:T(8,128)(2,1)}, bf16[4,256,128]{2,1,0:T(8,128)(2,1)}, f32[256,256]{1,0:T(8,128)S(1)}) custom-call(s32[2]{0:T(128)S(1)} %pad_add_fusion.1.pos_ref, s32[8]{0:T(128)S(1)} %copy-done.24, s32[8]{0:T(128)S(1)} %copy-done.26, ...), custom_call_target="tpu_custom_call" | custom-call | flops 1024 | bytes 1024 | tf_op jit(solution)/shard_map/prep/pallas_call | solution.py:85
  6.4 2.5 %collective-permute-start.11 = (bf16[4,256,128]{2,1,0:T(8,128)(2,1)}, bf16[4,256,128]{2,1,0:T(8,128)(2,1)S(1)}, u32[]{:S(2)}, u32[]{:S(2)}) collective-permute-start(bf16[4,256,128]{2,1,0:T(8,128)(2,1)} %get-tuple-element.79), channel_id=1, source_target_pairs={{0,8},{4,12},{8,0},{12,4},{1,9},{5,13},{9,1},{13,5},{2,10},{6,14},... | collective-permute-start | bytes 786440 | tf_op jit(solution)/shard_map/ppermute | solution.py:37
  9.1 6.0 %prep.6 = (bf16[4,256,256]{2,1,0:T(8,128)(2,1)S(1)}, bf16[4,256,256]{2,1,0:T(8,128)(2,1)}, bf16[4,256,256]{2,1,0:T(8,128)(2,1)}, bf16[4,256,256]{2,1,0:T(8,128)(2,1)}, f32[256,256]{1,0:T(8,128)S(1)}) custom-call(s32[2]{0:T(128)S(1)} %pad_add_fusion.1.pos_ref, s32[8]{0:T(128)S(1)} %copy-done.24, s32[8]{0:T(128)S(1)} %copy-done.26, ...), custom_call_target="tpu_custom_call" | custom-call | flops 1024 | bytes 1024 | tf_op jit(solution)/shard_map/prep/pallas_call | solution.py:85
  15.1 0.8 copy-done
  15.9 1.7 %collective-permute-start = (bf16[4,256,256]{2,1,0:T(8,128)(2,1)}, bf16[4,256,256]{2,1,0:T(8,128)(2,1)S(1)}, u32[]{:S(2)}, u32[]{:S(2)}) collective-permute-start(bf16[4,256,256]{2,1,0:T(8,128)(2,1)} %get-tuple-element.64), channel_id=1, source_target_pairs={{0,8},{4,12},{8,0},{12,4},{1,9},{5,13},{9,1},{13,5},{2,10},{6,14},... | collective-permute-start | bytes 1572872 | tf_op jit(solution)/shard_map/ppermute | solution.py:37
  19.0 5.8 %prep.7 = (bf16[4,256,256]{2,1,0:T(8,128)(2,1)S(1)}, bf16[4,256,256]{2,1,0:T(8,128)(2,1)S(1)}, bf16[4,256,256]{2,1,0:T(8,128)(2,1)}, bf16[4,256,256]{2,1,0:T(8,128)(2,1)}, f32[256,256]{1,0:T(8,128)S(1)}) custom-call(s32[2]{0:T(128)S(1)} %pad_add_fusion.1.pos_ref, s32[8]{0:T(128)S(1)} %copy-done.25, s32[8]{0:T(128)S(1)} %copy-done.27, ...), custom_call_target="tpu_custom_call" | custom-call | flops 1024 | bytes 1024 | tf_op jit(solution)/shard_map/prep/pallas_call | solution.py:85
  25.7 6.0 %prep.8 = (bf16[4,256,256]{2,1,0:T(8,128)(2,1)S(1)}, bf16[4,256,256]{2,1,0:T(8,128)(2,1)}, bf16[4,256,256]{2,1,0:T(8,128)(2,1)}, bf16[4,256,256]{2,1,0:T(8,128)(2,1)}, f32[256,256]{1,0:T(8,128)S(1)}) custom-call(s32[2]{0:T(128)S(1)} %pad_add_fusion.1.pos_ref, s32[8]{0:T(128)S(1)} %copy-done.25, s32[8]{0:T(128)S(1)} %copy-done.27, ...), custom_call_target="tpu_custom_call" | custom-call | flops 1024 | bytes 1024 | tf_op jit(solution)/shard_map/prep/pallas_call | solution.py:85
  32.6 3.3 %prep.9 = (bf16[4,256,128]{2,1,0:T(8,128)(2,1)S(1)}, bf16[4,256,128]{2,1,0:T(8,128)(2,1)S(1)}, bf16[4,256,128]{2,1,0:T(8,128)(2,1)S(1)}, bf16[4,256,128]{2,1,0:T(8,128)(2,1)S(1)}, f32[256,256]{1,0:T(8,128)S(1)}) custom-call(s32[2]{0:T(128)S(1)} %pad_add_fusion.1.pos_ref, s32[8]{0:T(128)S(1)} %copy-done.25, s32[8]{0:T(128)S(1)} %copy-done.27, ...), custom_call_target="tpu_custom_call" | custom-call | flops 1024 | bytes 1024 | tf_op jit(solution)/shard_map/prep/pallas_call | solution.py:85
  41.0 13.0 %multiply_convert_fusion.1 = (bf16[6,1,128,1024]{3,2,1,0:T(8,128)(2,1)S(1)}, bf16[6,1,128,1024]{3,2,1,0:T(8,128)(2,1)S(1)}) fusion(f32[1024]{0:T(1024)} %bitcast.27, f32[1024]{0:T(1024)S(1)} %bitcast.28, f32[6,128]{1,0:T(8,128)S(1)} %add_convert_fusion), kind=kLoop, calls=%fused_computation.5 | loop fusion | flops 5505024 | bytes 3156992 | tf_op jit(solution)/shard_map/convert
  54.0 1.2 copy-done.31
  58.4 1.7 %collective-permute-start.15 = (bf16[4,256,256]{2,1,0:T(8,128)(2,1)}, bf16[4,256,256]{2,1,0:T(8,128)(2,1)}, u32[]{:S(2)}, u32[]{:S(2)}) collective-permute-start(bf16[4,256,256]{2,1,0:T(8,128)(2,1)} %get-tuple-element.85), channel_id=1, source_target_pairs={{0,12},{4,8},{8,4},{12,0},{1,13},{5,9},{9,5},{13,1},{2,14},{6,10},... | collective-permute-start | bytes 1572872 | tf_op jit(solution)/shard_map/ppermute | solution.py:37
  60.5 0.8 copy-done.2
  61.3 0.8 copy-done.4
  62.1 0.8 copy-done.12
  63.1 1.8 %collective-permute-start.2 = (f32[12,256]{1,0:T(8,128)S(1)}, f32[12,256]{1,0:T(8,128)S(1)}, u32[]{:S(2)}, u32[]{:S(2)}) collective-permute-start(f32[12,256]{1,0:T(8,128)S(1)} %fusion.5), channel_id=1, source_target_pairs={{0,1},{1,0},{2,3},{3,2},{4,5},{5,4},{6,7},{7,6},{8,9},{9,8},{10,11... | collective-permute-start | bytes 36872 | tf_op jit(solution)/shard_map/ppermute | solution.py:46
  64.9 1.9 %collective-permute-done.2 = f32[12,256]{1,0:T(8,128)S(1)} collective-permute-done((f32[12,256]{1,0:T(8,128)S(1)}, f32[12,256]{1,0:T(8,128)S(1)}, u32[]{:S(2)}, u32[]{:S(2)}) %collective-permute-start.2) | collective-permute-done | bytes 12320 | tf_op jit(solution)/shard_map/ppermute | solution.py:46
  66.8 2.8 %collective-permute-start.3 = (f32[12,256]{1,0:T(8,128)S(1)}, f32[12,256]{1,0:T(8,128)S(1)}, u32[]{:S(2)}, u32[]{:S(2)}) collective-permute-start(f32[12,256]{1,0:T(8,128)S(1)} %add.103), channel_id=1, source_target_pairs={{0,2},{1,3},{2,0},{3,1},{4,6},{5,7},{6,4},{7,5},{8,10},{9,11},{10,... | collective-permute-start | bytes 36872 | tf_op jit(solution)/shard_map/ppermute | solution.py:46
  69.6 2.0 %collective-permute-done.3 = f32[12,256]{1,0:T(8,128)S(1)} collective-permute-done((f32[12,256]{1,0:T(8,128)S(1)}, f32[12,256]{1,0:T(8,128)S(1)}, u32[]{:S(2)}, u32[]{:S(2)}) %collective-permute-start.3) | collective-permute-done | bytes 12320 | tf_op jit(solution)/shard_map/ppermute | solution.py:46
  71.7 1.2 collective-permute-done.4
  72.8 1.5 %collective-permute-start.5 = (f32[12,256]{1,0:T(8,128)S(1)}, f32[12,256]{1,0:T(8,128)S(1)}, u32[]{:S(2)}, u32[]{:S(2)}) collective-permute-start(f32[12,256]{1,0:T(8,128)S(1)} %add.105), channel_id=1, source_target_pairs={{0,8},{4,12},{8,0},{12,4},{1,9},{5,13},{9,1},{13,5},{2,10},{6,14},... | collective-permute-start | bytes 36872 | tf_op jit(solution)/shard_map/ppermute | solution.py:46
  74.3 2.2 %pad_maximum_fusion.table_ref = bf16[6,2,128,1024]{3,2,1,0:T(8,128)(2,1)S(1)} fusion(bf16[6,1,128,1024]{3,2,1,0:T(8,128)(2,1)} %copy-done.32, bf16[6,1,128,1024]{3,2,1,0:T(8,128)(2,1)} %copy-done.31), kind=kLoop, calls=%fused_computation.2 | loop fusion | flops 1572864 | bytes 6291456 | tf_op jit(solution)/shard_map/stack | solution.py:209
  76.6 8.4 %collective-permute-done.5 = f32[12,256]{1,0:T(8,128)S(1)} collective-permute-done((f32[12,256]{1,0:T(8,128)S(1)}, f32[12,256]{1,0:T(8,128)S(1)}, u32[]{:S(2)}, u32[]{:S(2)}) %collective-permute-start.5) | collective-permute-done | bytes 12320 | tf_op jit(solution)/shard_map/ppermute | solution.py:46
  85.0 1.7 %collective-permute-start.17 = (bf16[4,256,256]{2,1,0:T(8,128)(2,1)}, bf16[4,256,256]{2,1,0:T(8,128)(2,1)}, u32[]{:S(2)}, u32[]{:S(2)}) collective-permute-start(bf16[4,256,256]{2,1,0:T(8,128)(2,1)} %get-tuple-element.89), channel_id=1, source_target_pairs={{0,8},{4,12},{8,0},{12,4},{1,9},{5,13},{9,1},{13,5},{2,10},{6,14},... | collective-permute-start | bytes 1572872 | tf_op jit(solution)/shard_map/ppermute | solution.py:37
  87.5 1.4 %collective-permute-start.10 = (bf16[4,256,128]{2,1,0:T(8,128)(2,1)}, bf16[4,256,128]{2,1,0:T(8,128)(2,1)}, u32[]{:S(2)}, u32[]{:S(2)}) collective-permute-start(bf16[4,256,128]{2,1,0:T(8,128)(2,1)} %copy-done.28), channel_id=1, source_target_pairs={{0,4},{4,0},{8,12},{12,8},{1,5},{5,1},{9,13},{13,9},{2,6},{6,2},{1... | collective-permute-start | bytes 786440 | tf_op jit(solution)/shard_map/ppermute | solution.py:37
  89.1 1.0 copy-done.15
  90.1 0.9 copy-done.17
  91.0 0.9 copy-done.19
  92.0 5.1 %band.5.rest_4_ = bf16[6,2,128,4,1024]{4,3,2,1,0:T(4,128)(2,1)} custom-call(f32[2,6]{1,0:T(2,128)S(1)} %divide_bitcast_fusion.coef_ref, bf16[6,2,128,1024]{3,2,1,0:T(8,128)(2,1)S(1)} %pad_maximum_fusion.table_ref, bf16[4,256,128]{2,1,0:T(8,128)(2,1)S(1)} %get-tuple-element.94.rest_0_, bf16[4,256,128]{2,1,0:T(8,128)(2,1)S(1)} %copy-done.15, ...), custom_call_target="tpu_custom_call" | custom-call | flops 1024 | bytes 1024 | tf_op jit(solution)/shard_map/band/pallas_call | solution.py:143
  97.1 7.1 %band.6.rest_4_ = bf16[6,2,128,4,1024]{4,3,2,1,0:T(4,128)(2,1)} custom-call(f32[2,6]{1,0:T(2,128)S(1)} %divide_bitcast_fusion.coef_ref, bf16[6,2,128,1024]{3,2,1,0:T(8,128)(2,1)S(1)} %pad_maximum_fusion.table_ref, bf16[4,256,256]{2,1,0:T(8,128)(2,1)S(1)} %copy-done.1, bf16[4,256,256]{2,1,0:T(8,128)(2,1)S(1)} %copy-done.7, ...), custom_call_target="tpu_custom_call", output_to_operand_aliasing={{}: (6, {})} | custom-call | flops 1024 | bytes 1024 | tf_op jit(solution)/shard_map/band/pallas_call | solution.py:143
  104.2 7.9 %band.7.rest_4_ = bf16[6,2,128,4,1024]{4,3,2,1,0:T(4,128)(2,1)} custom-call(f32[2,6]{1,0:T(2,128)S(1)} %divide_bitcast_fusion.coef_ref, bf16[6,2,128,1024]{3,2,1,0:T(8,128)(2,1)S(1)} %pad_maximum_fusion.table_ref, bf16[4,256,256]{2,1,0:T(8,128)(2,1)S(1)} %copy-done.11, bf16[4,256,256]{2,1,0:T(8,128)(2,1)S(1)} %copy-done.13, ...), custom_call_target="tpu_custom_call", output_to_operand_aliasing={{}: (6, {})} | custom-call | flops 1024 | bytes 1024 | tf_op jit(solution)/shard_map/band/pallas_call | solution.py:143
  112.1 8.0 %band.8.rest_4_ = bf16[6,2,128,4,1024]{4,3,2,1,0:T(4,128)(2,1)} custom-call(f32[2,6]{1,0:T(2,128)S(1)} %divide_bitcast_fusion.coef_ref, bf16[6,2,128,1024]{3,2,1,0:T(8,128)(2,1)S(1)} %pad_maximum_fusion.table_ref, bf16[4,256,256]{2,1,0:T(8,128)(2,1)S(1)} %copy-done.9, ...), custom_call_target="tpu_custom_call", output_to_operand_aliasing={{}: (6, {})} | custom-call | flops 1024 | bytes 1024 | tf_op jit(solution)/shard_map/band/pallas_call | solution.py:143
  120.1 5.6 %band.9 = bf16[6,2,128,4,1024]{4,3,2,1,0:T(4,128)(2,1)} custom-call(f32[2,6]{1,0:T(2,128)S(1)} %divide_bitcast_fusion.coef_ref, bf16[6,2,128,1024]{3,2,1,0:T(8,128)(2,1)S(1)} %pad_maximum_fusion.table_ref, bf16[4,256,128]{2,1,0:T(8,128)(2,1)S(1)} %copy-done.21, bf16[4,256,128]{2,1,0:T(8,128)(2,1)} %collective-permute-done.10.rest_1_, ...), custom_call_target="tpu_custom_call", output_to_operand_aliasing={{}: (6, {})} | custom-call | flops 1024 | bytes 1024 | tf_op jit(solution)/shard_map/band/pallas_call | solution.py:143
  (115 shorter events, 15.6 us)
Async XLA Ops:
  6.0 11.7 %collective-permute-start.6 = (bf16[4,256,128]{2,1,0:T(8,128)(2,1)S(1)}, bf16[4,256,128]{2,1,0:T(8,128)(2,1)S(1)}, u32[]{:S(2)}, u32[]{:S(2)}) collective-permute-start(bf16[4,256,128]{2,1,0:T(8,128)(2,1)S(1)} %get-tuple-element.72), channel_id=1, source_target_pairs={{0,4},{4,0},{8,12},{12,8},{1,5},{5,1},{9,13},{13,9},{2,6},{6,2},{1... | collective-permute-start | bytes 786440 | tf_op jit(solution)/shard_map/ppermute | solution.py:37
  6.4 50.6 %collective-permute-start.11 = (bf16[4,256,128]{2,1,0:T(8,128)(2,1)}, bf16[4,256,128]{2,1,0:T(8,128)(2,1)S(1)}, u32[]{:S(2)}, u32[]{:S(2)}) collective-permute-start(bf16[4,256,128]{2,1,0:T(8,128)(2,1)} %get-tuple-element.79), channel_id=1, source_target_pairs={{0,8},{4,12},{8,0},{12,4},{1,9},{5,13},{9,1},{13,5},{2,10},{6,14},... | collective-permute-start | bytes 786440 | tf_op jit(solution)/shard_map/ppermute | solution.py:37
  8.9 48.8 %collective-permute-start.14 = (bf16[4,256,128]{2,1,0:T(8,128)(2,1)}, bf16[4,256,128]{2,1,0:T(8,128)(2,1)S(1)}, u32[]{:S(2)}, u32[]{:S(2)}) collective-permute-start(bf16[4,256,128]{2,1,0:T(8,128)(2,1)} %get-tuple-element.84), channel_id=1, source_target_pairs={{0,12},{4,8},{8,4},{12,0},{1,13},{5,9},{9,5},{13,1},{2,14},{6,10},... | collective-permute-start | bytes 786440 | tf_op jit(solution)/shard_map/ppermute | solution.py:37
  9.1 9.9 %copy-start.23 = (s32[256]{0:T(256)S(1)}, s32[256]{0:T(256)}, u32[]{:S(2)}) copy-start(s32[256]{0:T(256)} %param.11) | copy-start | bytes 3076
  9.1 9.9 %copy-start.25 = (s32[8]{0:T(128)S(1)}, s32[8]{0:T(128)}, u32[]{:S(2)}) copy-start(s32[8]{0:T(128)} %off_ref.9) | copy-start | bytes 100
  9.1 9.9 %copy-start.27 = (s32[8]{0:T(128)S(1)}, s32[8]{0:T(128)}, u32[]{:S(2)}) copy-start(s32[8]{0:T(128)} %cnt_ref.9) | copy-start | bytes 100
  15.9 44.6 %collective-permute-start = (bf16[4,256,256]{2,1,0:T(8,128)(2,1)}, bf16[4,256,256]{2,1,0:T(8,128)(2,1)S(1)}, u32[]{:S(2)}, u32[]{:S(2)}) collective-permute-start(bf16[4,256,256]{2,1,0:T(8,128)(2,1)} %get-tuple-element.64), channel_id=1, source_target_pairs={{0,8},{4,12},{8,0},{12,4},{1,9},{5,13},{9,1},{13,5},{2,10},{6,14},... | collective-permute-start | bytes 1572872 | tf_op jit(solution)/shard_map/ppermute | solution.py:37
  17.6 43.7 %collective-permute-start.1 = (bf16[4,256,256]{2,1,0:T(8,128)(2,1)}, bf16[4,256,256]{2,1,0:T(8,128)(2,1)S(1)}, u32[]{:S(2)}, u32[]{:S(2)}) collective-permute-start(bf16[4,256,256]{2,1,0:T(8,128)(2,1)} %get-tuple-element.65), channel_id=1, source_target_pairs={{0,12},{4,8},{8,4},{12,0},{1,13},{5,9},{9,5},{13,1},{2,14},{6,10},... | collective-permute-start | bytes 1572872 | tf_op jit(solution)/shard_map/ppermute | solution.py:37
  18.4 21.7 %collective-permute-start.7 = (bf16[4,256,256]{2,1,0:T(8,128)(2,1)}, bf16[4,256,256]{2,1,0:T(8,128)(2,1)S(1)}, u32[]{:S(2)}, u32[]{:S(2)}) collective-permute-start(bf16[4,256,256]{2,1,0:T(8,128)(2,1)} %get-tuple-element.73), channel_id=1, source_target_pairs={{0,4},{4,0},{8,12},{12,8},{1,5},{5,1},{9,13},{13,9},{2,6},{6,2},{1... | collective-permute-start | bytes 1572872 | tf_op jit(solution)/shard_map/ppermute | solution.py:37
  32.5 6.7 %copy-start.33 = (f32[1024]{0:T(1024)S(1)}, f32[1024]{0:T(1024)}, u32[]{:S(2)}) copy-start(f32[1024]{0:T(1024)} %param.7) | copy-start | bytes 12292
  40.1 16.2 %copy-start.6 = (bf16[4,256,256]{2,1,0:T(8,128)(2,1)}, bf16[4,256,256]{2,1,0:T(8,128)(2,1)S(1)}, u32[]{:S(2)}) copy-start(bf16[4,256,256]{2,1,0:T(8,128)(2,1)S(1)} %collective-permute-done.7.rest_1_) | copy-start | bytes 1572868
  40.1 22.0 %collective-permute-start.8 = (bf16[4,256,256]{2,1,0:T(8,128)(2,1)S(1)}, bf16[4,256,256]{2,1,0:T(8,128)(2,1)S(1)}, u32[]{:S(2)}, u32[]{:S(2)}) collective-permute-start(bf16[4,256,256]{2,1,0:T(8,128)(2,1)S(1)} %get-tuple-element.74), channel_id=1, source_target_pairs={{0,4},{4,0},{8,12},{12,8},{1,5},{5,1},{9,13},{13,9},{2,6},{6,2},{1... | collective-permute-start | bytes 1572872 | tf_op jit(solution)/shard_map/ppermute | solution.py:37
  58.4 28.6 %collective-permute-start.15 = (bf16[4,256,256]{2,1,0:T(8,128)(2,1)}, bf16[4,256,256]{2,1,0:T(8,128)(2,1)}, u32[]{:S(2)}, u32[]{:S(2)}) collective-permute-start(bf16[4,256,256]{2,1,0:T(8,128)(2,1)} %get-tuple-element.85), channel_id=1, source_target_pairs={{0,12},{4,8},{8,4},{12,0},{1,13},{5,9},{9,5},{13,1},{2,14},{6,10},... | collective-permute-start | bytes 1572872 | tf_op jit(solution)/shard_map/ppermute | solution.py:37
  60.1 26.9 %collective-permute-start.12 = (bf16[4,256,256]{2,1,0:T(8,128)(2,1)}, bf16[4,256,256]{2,1,0:T(8,128)(2,1)}, u32[]{:S(2)}, u32[]{:S(2)}) collective-permute-start(bf16[4,256,256]{2,1,0:T(8,128)(2,1)} %get-tuple-element.80), channel_id=1, source_target_pairs={{0,8},{4,12},{8,0},{12,4},{1,9},{5,13},{9,1},{13,5},{2,10},{6,14},... | collective-permute-start | bytes 1572872 | tf_op jit(solution)/shard_map/ppermute | solution.py:37
  62.9 24.6 %collective-permute-start.9 = (bf16[4,256,256]{2,1,0:T(8,128)(2,1)}, bf16[4,256,256]{2,1,0:T(8,128)(2,1)}, u32[]{:S(2)}, u32[]{:S(2)}) collective-permute-start(bf16[4,256,256]{2,1,0:T(8,128)(2,1)} %get-tuple-element.75), channel_id=1, source_target_pairs={{0,4},{4,0},{8,12},{12,8},{1,5},{5,1},{9,13},{13,9},{2,6},{6,2},{1... | collective-permute-start | bytes 1572872 | tf_op jit(solution)/shard_map/ppermute | solution.py:37
  63.1 3.8 %collective-permute-start.2 = (f32[12,256]{1,0:T(8,128)S(1)}, f32[12,256]{1,0:T(8,128)S(1)}, u32[]{:S(2)}, u32[]{:S(2)}) collective-permute-start(f32[12,256]{1,0:T(8,128)S(1)} %fusion.5), channel_id=1, source_target_pairs={{0,1},{1,0},{2,3},{3,2},{4,5},{5,4},{6,7},{7,6},{8,9},{9,8},{10,11... | collective-permute-start | bytes 36872 | tf_op jit(solution)/shard_map/ppermute | solution.py:46
  66.8 4.8 %collective-permute-start.3 = (f32[12,256]{1,0:T(8,128)S(1)}, f32[12,256]{1,0:T(8,128)S(1)}, u32[]{:S(2)}, u32[]{:S(2)}) collective-permute-start(f32[12,256]{1,0:T(8,128)S(1)} %add.103), channel_id=1, source_target_pairs={{0,2},{1,3},{2,0},{3,1},{4,6},{5,7},{6,4},{7,5},{8,10},{9,11},{10,... | collective-permute-start | bytes 36872 | tf_op jit(solution)/shard_map/ppermute | solution.py:46
  71.6 1.2 collective-permute-start.4
  72.8 12.1 %collective-permute-start.5 = (f32[12,256]{1,0:T(8,128)S(1)}, f32[12,256]{1,0:T(8,128)S(1)}, u32[]{:S(2)}, u32[]{:S(2)}) collective-permute-start(f32[12,256]{1,0:T(8,128)S(1)} %add.105), channel_id=1, source_target_pairs={{0,8},{4,12},{8,0},{12,4},{1,9},{5,13},{9,1},{13,5},{2,10},{6,14},... | collective-permute-start | bytes 36872 | tf_op jit(solution)/shard_map/ppermute | solution.py:46
  76.5 35.6 %collective-permute-start.18 = (bf16[4,256,256]{2,1,0:T(8,128)(2,1)}, bf16[4,256,256]{2,1,0:T(8,128)(2,1)}, u32[]{:S(2)}, u32[]{:S(2)}) collective-permute-start(bf16[4,256,256]{2,1,0:T(8,128)(2,1)} %get-tuple-element.91), channel_id=1, source_target_pairs={{0,12},{4,8},{8,4},{12,0},{1,13},{5,9},{9,5},{13,1},{2,14},{6,10},... | collective-permute-start | bytes 1572872 | tf_op jit(solution)/shard_map/ppermute | solution.py:37
  85.0 27.1 %collective-permute-start.17 = (bf16[4,256,256]{2,1,0:T(8,128)(2,1)}, bf16[4,256,256]{2,1,0:T(8,128)(2,1)}, u32[]{:S(2)}, u32[]{:S(2)}) collective-permute-start(bf16[4,256,256]{2,1,0:T(8,128)(2,1)} %get-tuple-element.89), channel_id=1, source_target_pairs={{0,8},{4,12},{8,0},{12,4},{1,9},{5,13},{9,1},{13,5},{2,10},{6,14},... | collective-permute-start | bytes 1572872 | tf_op jit(solution)/shard_map/ppermute | solution.py:37
  87.0 33.1 %collective-permute-start.16 = (bf16[4,256,128]{2,1,0:T(8,128)(2,1)}, bf16[4,256,128]{2,1,0:T(8,128)(2,1)}, u32[]{:S(2)}, u32[]{:S(2)}) collective-permute-start(bf16[4,256,128]{2,1,0:T(8,128)(2,1)} %copy-done.30), channel_id=1, source_target_pairs={{0,12},{4,8},{8,4},{12,0},{1,13},{5,9},{9,5},{13,1},{2,14},{6,10},... | collective-permute-start | bytes 786440 | tf_op jit(solution)/shard_map/ppermute | solution.py:37
  87.1 33.0 %collective-permute-start.13 = (bf16[4,256,128]{2,1,0:T(8,128)(2,1)}, bf16[4,256,128]{2,1,0:T(8,128)(2,1)}, u32[]{:S(2)}, u32[]{:S(2)}) collective-permute-start(bf16[4,256,128]{2,1,0:T(8,128)(2,1)} %copy-done.29), channel_id=1, source_target_pairs={{0,8},{4,12},{8,0},{12,4},{1,9},{5,13},{9,1},{13,5},{2,10},{6,14},... | collective-permute-start | bytes 786440 | tf_op jit(solution)/shard_map/ppermute | solution.py:37
  87.5 32.6 %collective-permute-start.10 = (bf16[4,256,128]{2,1,0:T(8,128)(2,1)}, bf16[4,256,128]{2,1,0:T(8,128)(2,1)}, u32[]{:S(2)}, u32[]{:S(2)}) collective-permute-start(bf16[4,256,128]{2,1,0:T(8,128)(2,1)} %copy-done.28), channel_id=1, source_target_pairs={{0,4},{4,0},{8,12},{12,8},{1,5},{5,1},{9,13},{13,9},{2,6},{6,2},{1... | collective-permute-start | bytes 786440 | tf_op jit(solution)/shard_map/ppermute | solution.py:37
  92.0 5.1 %copy-start.1 = (bf16[4,256,256]{2,1,0:T(8,128)(2,1)S(1)}, bf16[4,256,256]{2,1,0:T(8,128)(2,1)}, u32[]{:S(2)}) copy-start(bf16[4,256,256]{2,1,0:T(8,128)(2,1)} %copy-done) | copy-start | bytes 1572868
  92.0 5.1 %copy-start.3 = (bf16[4,256,256]{2,1,0:T(8,128)(2,1)S(1)}, bf16[4,256,256]{2,1,0:T(8,128)(2,1)}, u32[]{:S(2)}) copy-start(bf16[4,256,256]{2,1,0:T(8,128)(2,1)} %copy-done.2) | copy-start | bytes 1572868
  92.0 5.1 %copy-start.5 = (bf16[4,256,256]{2,1,0:T(8,128)(2,1)S(1)}, bf16[4,256,256]{2,1,0:T(8,128)(2,1)}, u32[]{:S(2)}) copy-start(bf16[4,256,256]{2,1,0:T(8,128)(2,1)} %copy-done.4) | copy-start | bytes 1572868
  92.0 5.1 %copy-start.7 = (bf16[4,256,256]{2,1,0:T(8,128)(2,1)S(1)}, bf16[4,256,256]{2,1,0:T(8,128)(2,1)}, u32[]{:S(2)}) copy-start(bf16[4,256,256]{2,1,0:T(8,128)(2,1)} %copy-done.6) | copy-start | bytes 1572868
  97.1 7.1 %copy-start.11 = (bf16[4,256,256]{2,1,0:T(8,128)(2,1)S(1)}, bf16[4,256,256]{2,1,0:T(8,128)(2,1)}, u32[]{:S(2)}) copy-start(bf16[4,256,256]{2,1,0:T(8,128)(2,1)} %copy-done.10) | copy-start | bytes 1572868
  97.1 7.1 %copy-start.13 = (bf16[4,256,256]{2,1,0:T(8,128)(2,1)S(1)}, bf16[4,256,256]{2,1,0:T(8,128)(2,1)}, u32[]{:S(2)}) copy-start(bf16[4,256,256]{2,1,0:T(8,128)(2,1)} %copy-done.12) | copy-start | bytes 1572868
  104.2 7.9 %copy-start.9 = (bf16[4,256,256]{2,1,0:T(8,128)(2,1)S(1)}, bf16[4,256,256]{2,1,0:T(8,128)(2,1)}, u32[]{:S(2)}) copy-start(bf16[4,256,256]{2,1,0:T(8,128)(2,1)} %copy-done.8) | copy-start | bytes 1572868
  112.1 8.0 %copy-start.21 = (bf16[4,256,128]{2,1,0:T(8,128)(2,1)S(1)}, bf16[4,256,128]{2,1,0:T(8,128)(2,1)}, u32[]{:S(2)}) copy-start(bf16[4,256,128]{2,1,0:T(8,128)(2,1)} %copy-done.20) | copy-start | bytes 786436
  (21 other events, 17.5 us)

commit v3 on v2

--- a/solution.py
+++ b/solution.py
@@ -198,6 +198,7 @@
             far = [lax.optimization_barrier((p, q))[0] for p, q in zip(far, moved[k - 2][2:])]
         moved.append([parts[0], near[k]] + [send(p, 2 + i, n) for i, p in enumerate(far)])
 
+    (wavenumbers, band_start), _ = lax.optimization_barrier(((wavenumbers, band_start), moved[0][2:]))
     order = jnp.stack([source(me, s, n) for s in range(n)])
     frame_pos = (order[:, None] * frame_dev + jnp.arange(frame_dev, dtype=jnp.int32)[None, :]).reshape(-1)
     wave_set = jnp.take(wavenumbers.reshape(n, frame_dev), order, axis=0).reshape(-1)
@@ -210,8 +211,11 @@
         [jnp.cos(angle) * window, -jnp.sin(angle) * window], axis=1
     ).astype(jnp.bfloat16)
 
-    picked, _ = lax.optimization_barrier((picked, moved[min(1, chunks - 1)][2:]))
-    middle = table[:, :, NB // 2, :frame_dev].reshape(2 * ncav, frame_dev)
+    own = bins[:, NB // 2, None] * wave_set[None, :frame_dev] * TWO_PI
+    (own, picked), _ = lax.optimization_barrier(((own, picked), moved[min(1, chunks - 1)][2:]))
+    middle = jnp.stack(
+        [jnp.cos(own) * window[:frame_dev], -jnp.sin(own) * window[:frame_dev]], axis=1
+    ).astype(jnp.bfloat16).reshape(2 * ncav, frame_dev)
     part = jnp.dot(middle, picked.astype(jnp.bfloat16), preferred_element_type=jnp.float32)
     middle = total_over(total_over(part, "cols"), "wave").reshape(ncav, 2, -1)
     ref = jnp.sum(middle, axis=2)

time: 126 us -> 118 us (0.937)
  local copies, waits for them, and re-layouts: 18.4 us -> 12.2 us
  other arithmetic: 17.4 us -> 13.7 us
    unnamed x70, local copies, waits for them, and re-layouts: 16.9 us -> 11.1 us
    ppermute x15, waiting for transfers between devices: 0.04 us -> 3.09 us  [send(): lax.ppermute(value, 'wave', [(i, partner(i, step, n)) for i in range(n)])]
    ppermute x4, waiting for transfers between devices: 13.5 us -> 11.2 us  [total_over(): value = value + lax.ppermute(value, axis, [(i, i ^ step) for i in range(n)])]
    another operation x1, other arithmetic: 2.17 us -> 0.29 us  [shards(): jnp.stack([jnp.cos(angle) * window, -jnp.sin(angle) * window], axis=1)]
    another operation x1 -> x3, other arithmetic: 13 us -> 12.4 us
  transfers between devices with their start and end apart: 19 -> 19, of which waited for: 4 -> 3; matrix products, arithmetic and copies ran while one was open for 16% -> 13% of each run, Pallas kernels for 39% -> 42%
where the time goes in v3:
time: 118 us; the launch traced here: 117 us
  Pallas kernels  58.7 us (50%)
  starting transfers between devices  17.9 us (15%)
  waiting for transfers between devices  14.2 us (12%)
  other arithmetic  13.7 us (12%)
  local copies, waits for them, and re-layouts  12.2 us (10%)
    pallas_call x5, Pallas kernels, band(): pl.pallas_call(functools.partial(band_kernel, n), out_shape=out, grid=(nc...  33.7 us
    pallas_call x5, Pallas kernels, prep(): pl.pallas_call(functools.partial(prep_kernel, n, rows_dev, chunk, width_a...  25 us
    another operation x1, other arithmetic  12.3 us
    ppermute x15, starting transfers between devices, send(): lax.ppermute(value, 'wave', [(i, partner(i, step, n)) for i in range(n)])  11.3 us
    ppermute x4, waiting for transfers between devices, total_over(): value = value + lax.ppermute(value, axis, [(i, i ^ step) for i in range(n)])  11.2 us
    unnamed x70, local copies, waits for them, and re-layouts  11.1 us
    ppermute x4, starting transfers between devices, total_over(): value = value + lax.ppermute(value, axis, [(i, i ^ step) for i in range(n)])  6.66 us
    ppermute x15, waiting for transfers between devices, send(): lax.ppermute(value, 'wave', [(i, partner(i, step, n)) for i in range(n)])  3.09 us
  transfers between devices with their start and end apart: 19, of which 3 were waited for; matrix products, arithmetic and copies ran while one was open for 13% of the time, Pallas kernels for 42%

profile of v3, /device:TPU:0, one launch (start us, length us, event | category | flops | bytes accessed | tf_op | source)
XLA Modules:
  0.0 117.2 jit_solution(5317075836915156943)
XLA Ops:
  2.1 4.0 %prep.5 = (bf16[4,256,128]{2,1,0:T(8,128)(2,1)S(1)}, bf16[4,256,128]{2,1,0:T(8,128)(2,1)}, bf16[4,256,128]{2,1,0:T(8,128)(2,1)}, bf16[4,256,128]{2,1,0:T(8,128)(2,1)}, f32[256,256]{1,0:T(8,128)S(1)}) custom-call(s32[2]{0:T(128)S(1)} %pad_add_fusion.pos_ref, s32[8]{0:T(128)S(1)} %copy-done.24, s32[8]{0:T(128)S(1)} %copy-done.26, ...), custom_call_target="tpu_custom_call" | custom-call | flops 1024 | bytes 1024 | tf_op jit(solution)/shard_map/prep/pallas_call | solution.py:85
  6.1 2.9 %collective-permute-start = (bf16[4,256,128]{2,1,0:T(8,128)(2,1)}, bf16[4,256,128]{2,1,0:T(8,128)(2,1)S(1)}, u32[]{:S(2)}, u32[]{:S(2)}) collective-permute-start(bf16[4,256,128]{2,1,0:T(8,128)(2,1)} %get-tuple-element.53), channel_id=1, source_target_pairs={{0,8},{4,12},{8,0},{12,4},{1,9},{5,13},{9,1},{13,5},{2,10},{6,14},... | collective-permute-start | bytes 786440 | tf_op jit(solution)/shard_map/ppermute | solution.py:37
  9.1 5.8 %prep.6 = (bf16[4,256,256]{2,1,0:T(8,128)(2,1)S(1)}, bf16[4,256,256]{2,1,0:T(8,128)(2,1)S(1)}, bf16[4,256,256]{2,1,0:T(8,128)(2,1)}, bf16[4,256,256]{2,1,0:T(8,128)(2,1)}, f32[256,256]{1,0:T(8,128)S(1)}) custom-call(s32[2]{0:T(128)S(1)} %pad_add_fusion.pos_ref, s32[8]{0:T(128)S(1)} %copy-done.24, s32[8]{0:T(128)S(1)} %copy-done.26, ...), custom_call_target="tpu_custom_call" | custom-call | flops 1024 | bytes 1024 | tf_op jit(solution)/shard_map/prep/pallas_call | solution.py:85
  15.0 0.8 copy-done
  15.8 2.0 %collective-permute-start.2 = (bf16[4,256,256]{2,1,0:T(8,128)(2,1)}, bf16[4,256,256]{2,1,0:T(8,128)(2,1)S(1)}, u32[]{:S(2)}, u32[]{:S(2)}) collective-permute-start(bf16[4,256,256]{2,1,0:T(8,128)(2,1)} %get-tuple-element.71), channel_id=1, source_target_pairs={{0,8},{4,12},{8,0},{12,4},{1,9},{5,13},{9,1},{13,5},{2,10},{6,14},... | collective-permute-start | bytes 1572872 | tf_op jit(solution)/shard_map/ppermute | solution.py:37
  18.6 5.8 %prep.7 = (bf16[4,256,256]{2,1,0:T(8,128)(2,1)S(1)}, bf16[4,256,256]{2,1,0:T(8,128)(2,1)S(1)}, bf16[4,256,256]{2,1,0:T(8,128)(2,1)}, bf16[4,256,256]{2,1,0:T(8,128)(2,1)}, f32[256,256]{1,0:T(8,128)S(1)}) custom-call(s32[2]{0:T(128)S(1)} %pad_add_fusion.pos_ref, s32[8]{0:T(128)S(1)} %copy-done.25, s32[8]{0:T(128)S(1)} %copy-done.27, ...), custom_call_target="tpu_custom_call" | custom-call | flops 1024 | bytes 1024 | tf_op jit(solution)/shard_map/prep/pallas_call | solution.py:85
  24.4 0.8 copy-done.8
  25.3 6.0 %prep.8 = (bf16[4,256,256]{2,1,0:T(8,128)(2,1)S(1)}, bf16[4,256,256]{2,1,0:T(8,128)(2,1)}, bf16[4,256,256]{2,1,0:T(8,128)(2,1)}, bf16[4,256,256]{2,1,0:T(8,128)(2,1)}, f32[256,256]{1,0:T(8,128)S(1)}) custom-call(s32[2]{0:T(128)S(1)} %pad_add_fusion.pos_ref, s32[8]{0:T(128)S(1)} %copy-done.25, s32[8]{0:T(128)S(1)} %copy-done.27, ...), custom_call_target="tpu_custom_call" | custom-call | flops 1024 | bytes 1024 | tf_op jit(solution)/shard_map/prep/pallas_call | solution.py:85
  31.3 0.8 copy-done.6
  32.1 3.3 %prep.9 = (bf16[4,256,128]{2,1,0:T(8,128)(2,1)S(1)}, bf16[4,256,128]{2,1,0:T(8,128)(2,1)S(1)}, bf16[4,256,128]{2,1,0:T(8,128)(2,1)S(1)}, bf16[4,256,128]{2,1,0:T(8,128)(2,1)S(1)}, f32[256,256]{1,0:T(8,128)S(1)}) custom-call(s32[2]{0:T(128)S(1)} %pad_add_fusion.pos_ref, s32[8]{0:T(128)S(1)} %copy-done.25, s32[8]{0:T(128)S(1)} %copy-done.27, ...), custom_call_target="tpu_custom_call" | custom-call | flops 1024 | bytes 1024 | tf_op jit(solution)/shard_map/prep/pallas_call | solution.py:85
  36.3 0.7 copy-done.14
  37.0 0.7 copy-done.16
  38.4 0.7 copy-done.18
  39.9 3.1 %collective-permute-done.3.rest_3_ = bf16[4,256,256]{2,1,0:T(8,128)(2,1)S(1)} collective-permute-done((bf16[4,256,256]{2,1,0:T(8,128)(2,1)}, bf16[4,256,256]{2,1,0:T(8,128)(2,1)S(1)}, u32[]{:S(2)}, u32[]{:S(2)}) %collective-permute-start.3) | collective-permute-done | bytes 524320 | tf_op jit(solution)/shard_map/ppermute | solution.py:37
  43.0 0.9 copy-done.10
  44.6 1.9 %collective-permute-start.4 = (f32[12,256]{1,0:T(8,128)S(1)}, f32[12,256]{1,0:T(8,128)S(1)}, u32[]{:S(2)}, u32[]{:S(2)}) collective-permute-start(f32[12,256]{1,0:T(8,128)S(1)} %fusion.6), channel_id=1, source_target_pairs={{0,1},{1,0},{2,3},{3,2},{4,5},{5,4},{6,7},{7,6},{8,9},{9,8},{10,11... | collective-permute-start | bytes 36872 | tf_op jit(solution)/shard_map/ppermute | solution.py:46
  46.4 1.9 %collective-permute-done.4 = f32[12,256]{1,0:T(8,128)S(1)} collective-permute-done((f32[12,256]{1,0:T(8,128)S(1)}, f32[12,256]{1,0:T(8,128)S(1)}, u32[]{:S(2)}, u32[]{:S(2)}) %collective-permute-start.4) | collective-permute-done | bytes 12320 | tf_op jit(solution)/shard_map/ppermute | solution.py:46
  48.3 2.9 %collective-permute-start.5 = (f32[12,256]{1,0:T(8,128)S(1)}, f32[12,256]{1,0:T(8,128)S(1)}, u32[]{:S(2)}, u32[]{:S(2)}) collective-permute-start(f32[12,256]{1,0:T(8,128)S(1)} %add.103), channel_id=1, source_target_pairs={{0,2},{1,3},{2,0},{3,1},{4,6},{5,7},{6,4},{7,5},{8,10},{9,11},{10,... | collective-permute-start | bytes 36872 | tf_op jit(solution)/shard_map/ppermute | solution.py:46
  51.3 1.7 %collective-permute-start.13 = (bf16[4,256,256]{2,1,0:T(8,128)(2,1)}, bf16[4,256,256]{2,1,0:T(8,128)(2,1)}, u32[]{:S(2)}, u32[]{:S(2)}) collective-permute-start(bf16[4,256,256]{2,1,0:T(8,128)(2,1)} %get-tuple-element.87), channel_id=1, source_target_pairs={{0,8},{4,12},{8,0},{12,4},{1,9},{5,13},{9,1},{13,5},{2,10},{6,14},... | collective-permute-start | bytes 1572872 | tf_op jit(solution)/shard_map/ppermute | solution.py:37
  53.6 12.3 %multiply_convert_fusion.1 = (bf16[6,1,128,1024]{3,2,1,0:T(8,128)(2,1)S(1)}, bf16[6,1,128,1024]{3,2,1,0:T(8,128)(2,1)S(1)}) fusion(f32[1024]{0:T(1024)S(1)} %bitcast.33, f32[1024]{0:T(1024)S(1)} %bitcast.34, f32[6,128]{1,0:T(8,128)S(1)} %add_convert_fusion), kind=kLoop, calls=%fused_computation.3 | loop fusion | flops 5505024 | bytes 3156992 | tf_op jit(solution)/shard_map/convert
  65.9 1.7 %collective-permute-start.7 = (f32[12,256]{1,0:T(8,128)S(1)}, f32[12,256]{1,0:T(8,128)S(1)}, u32[]{:S(2)}, u32[]{:S(2)}) collective-permute-start(f32[12,256]{1,0:T(8,128)S(1)} %add.105), channel_id=1, source_target_pairs={{0,8},{4,12},{8,0},{12,4},{1,9},{5,13},{9,1},{13,5},{2,10},{6,14},... | collective-permute-start | bytes 36872 | tf_op jit(solution)/shard_map/ppermute | solution.py:46
  68.1 9.3 %collective-permute-done.7 = f32[12,256]{1,0:T(8,128)S(1)} collective-permute-done((f32[12,256]{1,0:T(8,128)S(1)}, f32[12,256]{1,0:T(8,128)S(1)}, u32[]{:S(2)}, u32[]{:S(2)}) %collective-permute-start.7) | collective-permute-done | bytes 12320 | tf_op jit(solution)/shard_map/ppermute | solution.py:46
  77.7 1.5 %collective-permute-start.16 = (bf16[4,256,128]{2,1,0:T(8,128)(2,1)}, bf16[4,256,128]{2,1,0:T(8,128)(2,1)}, u32[]{:S(2)}, u32[]{:S(2)}) collective-permute-start(bf16[4,256,128]{2,1,0:T(8,128)(2,1)} %copy-done.31), channel_id=1, source_target_pairs={{0,12},{4,8},{8,4},{12,0},{1,13},{5,9},{9,5},{13,1},{2,14},{6,10},... | collective-permute-start | bytes 786440 | tf_op jit(solution)/shard_map/ppermute | solution.py:37
  79.1 1.2 %collective-permute-start.14 = (bf16[4,256,128]{2,1,0:T(8,128)(2,1)}, bf16[4,256,128]{2,1,0:T(8,128)(2,1)}, u32[]{:S(2)}, u32[]{:S(2)}) collective-permute-start(bf16[4,256,128]{2,1,0:T(8,128)(2,1)} %copy-done.30), channel_id=1, source_target_pairs={{0,8},{4,12},{8,0},{12,4},{1,9},{5,13},{9,1},{13,5},{2,10},{6,14},... | collective-permute-start | bytes 786440 | tf_op jit(solution)/shard_map/ppermute | solution.py:37
  80.5 1.0 copy-done.15
  81.5 0.9 copy-done.17
  82.4 0.9 copy-done.19
  83.4 5.1 %band.5.rest_4_ = bf16[6,2,128,4,1024]{4,3,2,1,0:T(4,128)(2,1)} custom-call(f32[2,6]{1,0:T(2,128)S(1)} %divide_bitcast_fusion.coef_ref, bf16[6,2,128,1024]{3,2,1,0:T(8,128)(2,1)S(1)} %pad_maximum_fusion.table_ref, bf16[4,256,128]{2,1,0:T(8,128)(2,1)S(1)} %get-tuple-element.100.rest_0_, bf16[4,256,128]{2,1,0:T(8,128)(2,1)S(1)} %copy-done.19, ...), custom_call_target="tpu_custom_call" | custom-call | flops 1024 | bytes 1024 | tf_op jit(solution)/shard_map/band/pallas_call | solution.py:143
  88.5 7.1 %band.6.rest_4_ = bf16[6,2,128,4,1024]{4,3,2,1,0:T(4,128)(2,1)} custom-call(f32[2,6]{1,0:T(2,128)S(1)} %divide_bitcast_fusion.coef_ref, bf16[6,2,128,1024]{3,2,1,0:T(8,128)(2,1)S(1)} %pad_maximum_fusion.table_ref, bf16[4,256,256]{2,1,0:T(8,128)(2,1)S(1)} %copy-done.1, bf16[4,256,256]{2,1,0:T(8,128)(2,1)S(1)} %copy-done.11, ...), custom_call_target="tpu_custom_call", output_to_operand_aliasing={{}: (6, {})} | custom-call | flops 1024 | bytes 1024 | tf_op jit(solution)/shard_map/band/pallas_call | solution.py:143
  95.6 7.9 %band.7.rest_4_ = bf16[6,2,128,4,1024]{4,3,2,1,0:T(4,128)(2,1)} custom-call(f32[2,6]{1,0:T(2,128)S(1)} %divide_bitcast_fusion.coef_ref, bf16[6,2,128,1024]{3,2,1,0:T(8,128)(2,1)S(1)} %pad_maximum_fusion.table_ref, bf16[4,256,256]{2,1,0:T(8,128)(2,1)S(1)} %copy-done.9, bf16[4,256,256]{2,1,0:T(8,128)(2,1)S(1)} %copy-done.13, ...), custom_call_target="tpu_custom_call", output_to_operand_aliasing={{}: (6, {})} | custom-call | flops 1024 | bytes 1024 | tf_op jit(solution)/shard_map/band/pallas_call | solution.py:143
  103.5 8.0 %band.8.rest_4_ = bf16[6,2,128,4,1024]{4,3,2,1,0:T(4,128)(2,1)} custom-call(f32[2,6]{1,0:T(2,128)S(1)} %divide_bitcast_fusion.coef_ref, bf16[6,2,128,1024]{3,2,1,0:T(8,128)(2,1)S(1)} %pad_maximum_fusion.table_ref, bf16[4,256,256]{2,1,0:T(8,128)(2,1)S(1)} %copy-done.7, ...), custom_call_target="tpu_custom_call", output_to_operand_aliasing={{}: (6, {})} | custom-call | flops 1024 | bytes 1024 | tf_op jit(solution)/shard_map/band/pallas_call | solution.py:143
  111.5 5.6 %band.9 = bf16[6,2,128,4,1024]{4,3,2,1,0:T(4,128)(2,1)} custom-call(f32[2,6]{1,0:T(2,128)S(1)} %divide_bitcast_fusion.coef_ref, bf16[6,2,128,1024]{3,2,1,0:T(8,128)(2,1)S(1)} %pad_maximum_fusion.table_ref, bf16[4,256,128]{2,1,0:T(8,128)(2,1)S(1)} %copy-done.21, bf16[4,256,128]{2,1,0:T(8,128)(2,1)} %collective-permute-done.12.rest_1_, ...), custom_call_target="tpu_custom_call", output_to_operand_aliasing={{}: (6, {})} | custom-call | flops 1024 | bytes 1024 | tf_op jit(solution)/shard_map/band/pallas_call | solution.py:143
  (122 shorter events, 7.7 us)
Async XLA Ops:
  6.1 29.5 %collective-permute-start = (bf16[4,256,128]{2,1,0:T(8,128)(2,1)}, bf16[4,256,128]{2,1,0:T(8,128)(2,1)S(1)}, u32[]{:S(2)}, u32[]{:S(2)}) collective-permute-start(bf16[4,256,128]{2,1,0:T(8,128)(2,1)} %get-tuple-element.53), channel_id=1, source_target_pairs={{0,8},{4,12},{8,0},{12,4},{1,9},{5,13},{9,1},{13,5},{2,10},{6,14},... | collective-permute-start | bytes 786440 | tf_op jit(solution)/shard_map/ppermute | solution.py:37
  9.0 28.0 %collective-permute-start.1 = (bf16[4,256,128]{2,1,0:T(8,128)(2,1)}, bf16[4,256,128]{2,1,0:T(8,128)(2,1)S(1)}, u32[]{:S(2)}, u32[]{:S(2)}) collective-permute-start(bf16[4,256,128]{2,1,0:T(8,128)(2,1)} %get-tuple-element.54), channel_id=1, source_target_pairs={{0,12},{4,8},{8,4},{12,0},{1,13},{5,9},{9,5},{13,1},{2,14},{6,10},... | collective-permute-start | bytes 786440 | tf_op jit(solution)/shard_map/ppermute | solution.py:37
  9.0 29.4 %collective-permute-start.8 = (bf16[4,256,128]{2,1,0:T(8,128)(2,1)}, bf16[4,256,128]{2,1,0:T(8,128)(2,1)S(1)}, u32[]{:S(2)}, u32[]{:S(2)}) collective-permute-start(bf16[4,256,128]{2,1,0:T(8,128)(2,1)} %get-tuple-element.80), channel_id=1, source_target_pairs={{0,4},{4,0},{8,12},{12,8},{1,5},{5,1},{9,13},{13,9},{2,6},{6,2},{1... | collective-permute-start | bytes 786440 | tf_op jit(solution)/shard_map/ppermute | solution.py:37
  9.1 9.4 %copy-start.23 = (s32[256]{0:T(256)S(1)}, s32[256]{0:T(256)}, u32[]{:S(2)}) copy-start(s32[256]{0:T(256)} %param.11) | copy-start | bytes 3076
  9.1 9.4 %copy-start.25 = (s32[8]{0:T(128)S(1)}, s32[8]{0:T(128)}, u32[]{:S(2)}) copy-start(s32[8]{0:T(128)} %off_ref.9) | copy-start | bytes 100
  9.1 9.4 %copy-start.27 = (s32[8]{0:T(128)S(1)}, s32[8]{0:T(128)}, u32[]{:S(2)}) copy-start(s32[8]{0:T(128)} %cnt_ref.9) | copy-start | bytes 100
  15.8 24.1 %collective-permute-start.2 = (bf16[4,256,256]{2,1,0:T(8,128)(2,1)}, bf16[4,256,256]{2,1,0:T(8,128)(2,1)S(1)}, u32[]{:S(2)}, u32[]{:S(2)}) collective-permute-start(bf16[4,256,256]{2,1,0:T(8,128)(2,1)} %get-tuple-element.71), channel_id=1, source_target_pairs={{0,8},{4,12},{8,0},{12,4},{1,9},{5,13},{9,1},{13,5},{2,10},{6,14},... | collective-permute-start | bytes 1572872 | tf_op jit(solution)/shard_map/ppermute | solution.py:37
  17.8 25.2 %collective-permute-start.3 = (bf16[4,256,256]{2,1,0:T(8,128)(2,1)}, bf16[4,256,256]{2,1,0:T(8,128)(2,1)S(1)}, u32[]{:S(2)}, u32[]{:S(2)}) collective-permute-start(bf16[4,256,256]{2,1,0:T(8,128)(2,1)} %get-tuple-element.72), channel_id=1, source_target_pairs={{0,12},{4,8},{8,4},{12,0},{1,13},{5,9},{9,5},{13,1},{2,14},{6,10},... | collective-permute-start | bytes 1572872 | tf_op jit(solution)/shard_map/ppermute | solution.py:37
  32.1 5.6 %copy-start.32 = (f32[1024]{0:T(1024)S(1)}, f32[1024]{0:T(1024)}, u32[]{:S(2)}) copy-start(f32[1024]{0:T(1024)} %param.7) | copy-start | bytes 12292
  32.1 7.5 %copy-start.33 = (s32[6]{0:T(128)S(1)}, s32[6]{0:T(128)}, u32[]{:S(2)}) copy-start(s32[6]{0:T(128)} %param.8) | copy-start | bytes 76
  35.5 32.2 %copy-start.31 = (bf16[4,256,128]{2,1,0:T(8,128)(2,1)}, bf16[4,256,128]{2,1,0:T(8,128)(2,1)S(1)}, u32[]{:S(2)}) copy-start(bf16[4,256,128]{2,1,0:T(8,128)(2,1)S(1)} %get-tuple-element.92) | copy-start | bytes 786436
  39.1 3.9 %collective-permute-start.9 = (bf16[4,256,256]{2,1,0:T(8,128)(2,1)}, bf16[4,256,256]{2,1,0:T(8,128)(2,1)S(1)}, u32[]{:S(2)}, u32[]{:S(2)}) collective-permute-start(bf16[4,256,256]{2,1,0:T(8,128)(2,1)} %copy-done.28), channel_id=1, source_target_pairs={{0,4},{4,0},{8,12},{12,8},{1,5},{5,1},{9,13},{13,9},{2,6},{6,2},{1... | collective-permute-start | bytes 1572872 | tf_op jit(solution)/shard_map/ppermute | solution.py:37
  39.9 27.8 %copy-start.2 = (bf16[4,256,256]{2,1,0:T(8,128)(2,1)}, bf16[4,256,256]{2,1,0:T(8,128)(2,1)S(1)}, u32[]{:S(2)}) copy-start(bf16[4,256,256]{2,1,0:T(8,128)(2,1)S(1)} %collective-permute-done.2.rest_2_) | copy-start | bytes 1572868
  43.0 24.7 %copy-start.4 = (bf16[4,256,256]{2,1,0:T(8,128)(2,1)}, bf16[4,256,256]{2,1,0:T(8,128)(2,1)S(1)}, u32[]{:S(2)}) copy-start(bf16[4,256,256]{2,1,0:T(8,128)(2,1)S(1)} %collective-permute-done.3.rest_3_) | copy-start | bytes 1572868
  44.0 9.3 %collective-permute-start.10 = (bf16[4,256,256]{2,1,0:T(8,128)(2,1)S(1)}, bf16[4,256,256]{2,1,0:T(8,128)(2,1)S(1)}, u32[]{:S(2)}, u32[]{:S(2)}) collective-permute-start(bf16[4,256,256]{2,1,0:T(8,128)(2,1)S(1)} %get-tuple-element.82), channel_id=1, source_target_pairs={{0,4},{4,0},{8,12},{12,8},{1,5},{5,1},{9,13},{13,9},{2,6},{6,2},{1... | collective-permute-start | bytes 1572872 | tf_op jit(solution)/shard_map/ppermute | solution.py:37
  44.6 3.8 %collective-permute-start.4 = (f32[12,256]{1,0:T(8,128)S(1)}, f32[12,256]{1,0:T(8,128)S(1)}, u32[]{:S(2)}, u32[]{:S(2)}) collective-permute-start(f32[12,256]{1,0:T(8,128)S(1)} %fusion.6), channel_id=1, source_target_pairs={{0,1},{1,0},{2,3},{3,2},{4,5},{5,4},{6,7},{7,6},{8,9},{9,8},{10,11... | collective-permute-start | bytes 36872 | tf_op jit(solution)/shard_map/ppermute | solution.py:46
  48.3 4.7 %collective-permute-start.5 = (f32[12,256]{1,0:T(8,128)S(1)}, f32[12,256]{1,0:T(8,128)S(1)}, u32[]{:S(2)}, u32[]{:S(2)}) collective-permute-start(f32[12,256]{1,0:T(8,128)S(1)} %add.103), channel_id=1, source_target_pairs={{0,2},{1,3},{2,0},{3,1},{4,6},{5,7},{6,4},{7,5},{8,10},{9,11},{10,... | collective-permute-start | bytes 36872 | tf_op jit(solution)/shard_map/ppermute | solution.py:46
  51.3 26.4 %collective-permute-start.15 = (bf16[4,256,256]{2,1,0:T(8,128)(2,1)}, bf16[4,256,256]{2,1,0:T(8,128)(2,1)}, u32[]{:S(2)}, u32[]{:S(2)}) collective-permute-start(bf16[4,256,256]{2,1,0:T(8,128)(2,1)} %get-tuple-element.91), channel_id=1, source_target_pairs={{0,12},{4,8},{8,4},{12,0},{1,13},{5,9},{9,5},{13,1},{2,14},{6,10},... | collective-permute-start | bytes 1572872 | tf_op jit(solution)/shard_map/ppermute | solution.py:37
  51.3 26.4 %collective-permute-start.13 = (bf16[4,256,256]{2,1,0:T(8,128)(2,1)}, bf16[4,256,256]{2,1,0:T(8,128)(2,1)}, u32[]{:S(2)}, u32[]{:S(2)}) collective-permute-start(bf16[4,256,256]{2,1,0:T(8,128)(2,1)} %get-tuple-element.87), channel_id=1, source_target_pairs={{0,8},{4,12},{8,0},{12,4},{1,9},{5,13},{9,1},{13,5},{2,10},{6,14},... | collective-permute-start | bytes 1572872 | tf_op jit(solution)/shard_map/ppermute | solution.py:37
  53.0 12.9 %collective-permute-start.6 = (f32[12,256]{1,0:T(8,128)S(1)}, f32[12,256]{1,0:T(8,128)S(1)}, u32[]{:S(2)}, u32[]{:S(2)}) collective-permute-start(f32[12,256]{1,0:T(8,128)S(1)} %add.104), channel_id=1, source_target_pairs={{0,4},{4,0},{8,12},{12,8},{1,5},{5,1},{9,13},{13,9},{2,6},{6,2},{1... | collective-permute-start | bytes 36872 | tf_op jit(solution)/shard_map/ppermute | solution.py:46
  53.2 14.4 %copy-start.12 = (bf16[4,256,256]{2,1,0:T(8,128)(2,1)}, bf16[4,256,256]{2,1,0:T(8,128)(2,1)S(1)}, u32[]{:S(2)}) copy-start(bf16[4,256,256]{2,1,0:T(8,128)(2,1)S(1)} %collective-permute-done.10.rest_1_) | copy-start | bytes 1572868
  53.2 27.1 %collective-permute-start.11 = (bf16[4,256,256]{2,1,0:T(8,128)(2,1)}, bf16[4,256,256]{2,1,0:T(8,128)(2,1)}, u32[]{:S(2)}, u32[]{:S(2)}) collective-permute-start(bf16[4,256,256]{2,1,0:T(8,128)(2,1)} %get-tuple-element.83), channel_id=1, source_target_pairs={{0,4},{4,0},{8,12},{12,8},{1,5},{5,1},{9,13},{13,9},{2,6},{6,2},{1... | collective-permute-start | bytes 1572872 | tf_op jit(solution)/shard_map/ppermute | solution.py:37
  65.9 11.4 %collective-permute-start.7 = (f32[12,256]{1,0:T(8,128)S(1)}, f32[12,256]{1,0:T(8,128)S(1)}, u32[]{:S(2)}, u32[]{:S(2)}) collective-permute-start(f32[12,256]{1,0:T(8,128)S(1)} %add.105), channel_id=1, source_target_pairs={{0,8},{4,12},{8,0},{12,4},{1,9},{5,13},{9,1},{13,5},{2,10},{6,14},... | collective-permute-start | bytes 36872 | tf_op jit(solution)/shard_map/ppermute | solution.py:46
  68.0 35.5 %collective-permute-start.18 = (bf16[4,256,256]{2,1,0:T(8,128)(2,1)}, bf16[4,256,256]{2,1,0:T(8,128)(2,1)}, u32[]{:S(2)}, u32[]{:S(2)}) collective-permute-start(bf16[4,256,256]{2,1,0:T(8,128)(2,1)} %get-tuple-element.97), channel_id=1, source_target_pairs={{0,12},{4,8},{8,4},{12,0},{1,13},{5,9},{9,5},{13,1},{2,14},{6,10},... | collective-permute-start | bytes 1572872 | tf_op jit(solution)/shard_map/ppermute | solution.py:37
  77.3 26.2 %collective-permute-start.17 = (bf16[4,256,256]{2,1,0:T(8,128)(2,1)}, bf16[4,256,256]{2,1,0:T(8,128)(2,1)}, u32[]{:S(2)}, u32[]{:S(2)}) collective-permute-start(bf16[4,256,256]{2,1,0:T(8,128)(2,1)} %get-tuple-element.95), channel_id=1, source_target_pairs={{0,8},{4,12},{8,0},{12,4},{1,9},{5,13},{9,1},{13,5},{2,10},{6,14},... | collective-permute-start | bytes 1572872 | tf_op jit(solution)/shard_map/ppermute | solution.py:37
  77.7 33.9 %collective-permute-start.16 = (bf16[4,256,128]{2,1,0:T(8,128)(2,1)}, bf16[4,256,128]{2,1,0:T(8,128)(2,1)}, u32[]{:S(2)}, u32[]{:S(2)}) collective-permute-start(bf16[4,256,128]{2,1,0:T(8,128)(2,1)} %copy-done.31), channel_id=1, source_target_pairs={{0,12},{4,8},{8,4},{12,0},{1,13},{5,9},{9,5},{13,1},{2,14},{6,10},... | collective-permute-start | bytes 786440 | tf_op jit(solution)/shard_map/ppermute | solution.py:37
  79.1 32.4 %collective-permute-start.14 = (bf16[4,256,128]{2,1,0:T(8,128)(2,1)}, bf16[4,256,128]{2,1,0:T(8,128)(2,1)}, u32[]{:S(2)}, u32[]{:S(2)}) collective-permute-start(bf16[4,256,128]{2,1,0:T(8,128)(2,1)} %copy-done.30), channel_id=1, source_target_pairs={{0,8},{4,12},{8,0},{12,4},{1,9},{5,13},{9,1},{13,5},{2,10},{6,14},... | collective-permute-start | bytes 786440 | tf_op jit(solution)/shard_map/ppermute | solution.py:37
  80.3 31.2 %collective-permute-start.12 = (bf16[4,256,128]{2,1,0:T(8,128)(2,1)}, bf16[4,256,128]{2,1,0:T(8,128)(2,1)}, u32[]{:S(2)}, u32[]{:S(2)}) collective-permute-start(bf16[4,256,128]{2,1,0:T(8,128)(2,1)} %copy-done.29), channel_id=1, source_target_pairs={{0,4},{4,0},{8,12},{12,8},{1,5},{5,1},{9,13},{13,9},{2,6},{6,2},{1... | collective-permute-start | bytes 786440 | tf_op jit(solution)/shard_map/ppermute | solution.py:37
  88.5 7.1 %copy-start.9 = (bf16[4,256,256]{2,1,0:T(8,128)(2,1)S(1)}, bf16[4,256,256]{2,1,0:T(8,128)(2,1)}, u32[]{:S(2)}) copy-start(bf16[4,256,256]{2,1,0:T(8,128)(2,1)} %copy-done.8) | copy-start | bytes 1572868
  88.5 7.1 %copy-start.13 = (bf16[4,256,256]{2,1,0:T(8,128)(2,1)S(1)}, bf16[4,256,256]{2,1,0:T(8,128)(2,1)}, u32[]{:S(2)}) copy-start(bf16[4,256,256]{2,1,0:T(8,128)(2,1)} %copy-done.12) | copy-start | bytes 1572868
  95.6 7.9 %copy-start.7 = (bf16[4,256,256]{2,1,0:T(8,128)(2,1)S(1)}, bf16[4,256,256]{2,1,0:T(8,128)(2,1)}, u32[]{:S(2)}) copy-start(bf16[4,256,256]{2,1,0:T(8,128)(2,1)} %copy-done.6) | copy-start | bytes 1572868
  103.5 8.0 %copy-start.21 = (bf16[4,256,128]{2,1,0:T(8,128)(2,1)S(1)}, bf16[4,256,128]{2,1,0:T(8,128)(2,1)}, u32[]{:S(2)}) copy-start(bf16[4,256,128]{2,1,0:T(8,128)(2,1)} %copy-done.20) | copy-start | bytes 786436
  (21 other events, 34.9 us)
